TPU v7x, 512 devices: a whole 4x8x8 slice. The times are simulated.
512 devices in a mesh: wide: 64 (over z_lo, y, core), narrow: 8 (over z_hi, x).
Axes of the slice: x: 4, y: 8, z: 8 (z_hi: 2, z_lo: 4; z = z_hi * 4 + z_lo), core: 2. Of those that a mesh axis runs over, the one named last changes fastest.
Arguments:
- density: bfloat16 [128, 64, 32, 192], P('wide', 'narrow'), may hold values from -6 to 6
- analysis_weight: bfloat16 [5, 5, 5, 192, 192], P(None, None, None, 'narrow'), may hold values from -0.0390625 to 0.0390625
- analysis_bias: float32 [192], replicated, may hold values from -3 to 3
- norm_beta: float32 [192], replicated, may hold values from 0.5 to 2
- norm_gamma: float32 [192, 192], replicated, may hold values from 0.0001 to 0.1
- hyper_weight: bfloat16 [3, 3, 3, 192, 192], P(None, None, None, 'narrow'), may hold values from -0.078125 to 0.078125
- hyper_bias: float32 [192], replicated, may hold values from -3 to 3
- synthesis_weight: bfloat16 [3, 3, 3, 192, 192], P(None, None, None, 'narrow'), may hold values from -0.078125 to 0.078125
- synthesis_bias: float32 [192], replicated, may hold values from -4 to 4
Outputs:
- latent: bfloat16 [64, 32, 16, 192], P('wide', 'narrow')
- scales: float32 [64, 32, 16, 192], P('wide', 'narrow')
All inputs are finite; a program needn't handle non-finite values.
Results may differ from a plain program's by a relative error of at most 0.0034.
Values may be sent and summed in bfloat16 or wider, within the bound.
A program may use at most 64 MiB of HBM per device.

v0:
```python
import jax
import jax.numpy as jnp
from jax import lax
from jax.sharding import PartitionSpec as P


def padded_2(array, sides, width):
    for axis, dim in sides:
        size, length = (lax.axis_size(axis), array.shape[dim])
        up = [(i, (i + 1) % size) for i in range(size - 1)]
        down = [(j, i) for i, j in up]
        last = lax.slice_in_dim(array, length - width, length, axis=dim)
        leading = lax.slice_in_dim(array, 0, width, axis=dim)
        before = lax.ppermute(last, axis, up)
        after = lax.ppermute(leading, axis, down)
        array = jnp.concatenate([before, array, after], axis=dim)
    return array


def normalize(conv_out, norm_beta, norm_gamma):
    denom = norm_beta + jnp.dot(conv_out * conv_out, norm_gamma, precision=lax.Precision.HIGHEST)
    return conv_out * lax.rsqrt(denom)


def strided_conv(padded, weight, out_rows, out_cols):
    outputs = weight.shape[-1]
    total = jnp.zeros((1, out_rows, out_cols, outputs), jnp.float32)
    for first in range(5):
        plane = padded[first : first + 1]
        stacked = jnp.concatenate(
            [
                plane[
                    :, second : second + 2 * out_rows - 1 : 2, third : third + 2 * out_cols - 1 : 2
                ]
                for second in range(5)
                for third in range(5)
            ],
            axis=3,
        )
        kernel = weight[first].reshape(-1, outputs)
        total = total + jnp.dot(stacked, kernel, preferred_element_type=jnp.float32)
    return total


def cube_conv(extended, weight):
    padded = jnp.pad(extended, ((0, 0), (0, 0), (1, 1), (0, 0)))
    planes = padded.shape[0] - 2
    out_rows = padded.shape[1] - 2
    out_cols = padded.shape[2] - 2
    outputs = weight.shape[-1]
    total = jnp.zeros((planes, out_rows, out_cols, outputs), jnp.float32)
    for first in range(3):
        for second in range(3):
            rows = padded[first : first + planes, second : second + out_rows]
            stacked = jnp.concatenate(
                [rows[:, :, third : third + out_cols] for third in range(3)], axis=3
            )
            kernel = weight[first, second].reshape(-1, outputs)
            total = total + jnp.dot(stacked, kernel, preferred_element_type=jnp.float32)
    return total


def on_device(
    density,
    analysis_weight,
    analysis_bias,
    norm_beta,
    norm_gamma,
    hyper_weight,
    hyper_bias,
    synthesis_weight,
    synthesis_bias,
):
    out_rows = density.shape[1] // 2
    out_cols = density.shape[2] // 2
    padded = padded_2(density, (("wide", 0), ("narrow", 1)), 2)
    padded = jnp.pad(padded, ((0, 0), (0, 0), (2, 2), (0, 0)))
    conv_out = strided_conv(
        padded, lax.all_gather(analysis_weight, "narrow", axis=3, tiled=True), out_rows, out_cols
    )
    conv_out = conv_out + analysis_bias
    latent = normalize(conv_out, norm_beta, norm_gamma).astype(jnp.bfloat16)
    kernels = (
        lax.all_gather(hyper_weight, "narrow", axis=3, tiled=True),
        lax.all_gather(synthesis_weight, "narrow", axis=3, tiled=True),
    )
    latent_ext = padded_2(latent, (("wide", 0), ("narrow", 1)), 1)
    hidden = jax.nn.relu(cube_conv(jnp.abs(latent_ext), kernels[0]) + hyper_bias).astype(
        jnp.bfloat16
    )
    hidden_ext = padded_2(hidden, (("wide", 0), ("narrow", 1)), 1)
    scales = 0.11 + jax.nn.softplus(cube_conv(hidden_ext, kernels[1]) + synthesis_bias)
    return (latent, scales)


def solution(mesh):
    in_specs = (
        P("wide", "narrow", None, None),
        P(None, None, None, "narrow", None),
        P(),
        P(),
        P(),
        P(None, None, None, "narrow", None),
        P(),
        P(None, None, None, "narrow", None),
        P(),
    )
    out_specs = (P("wide", "narrow", None, None), P("wide", "narrow", None, None))
    return jax.shard_map(
        on_device, mesh=mesh, in_specs=in_specs, out_specs=out_specs, check_vma=False
    )
```

profile of v0, /device:TPU:1, one launch (start us, length us, event | category | flops | bytes accessed | tf_op | source)
XLA Modules:
  0.0 452.8 jit_solution(5328047861193033787)
XLA Ops:
  8.7 4.6 %collective-permute-start = (bf16[2,8,32,192]{3,2,1,0:T(8,128)(2,1)}, bf16[2,8,32,192]{3,2,1,0:T(8,128)(2,1)S(1)}, u32[]{:S(2)}, u32[]{:S(2)}) collective-permute-start(bf16[2,8,32,192]{3,2,1,0:T(8,128)(2,1)} %param.9), channel_id=1, source_target_pairs={{0,8},{8,16},{16,24},{24,32},{32,40},{40,48},{48,56},{56,64},{64,7... | collective-permute-start | bytes 589832 | tf_op jit(solution)/shard_map/ppermute | solution.py:14
  13.3 5.5 %collective-permute-start.1 = (bf16[2,8,32,192]{3,2,1,0:T(8,128)(2,1)}, bf16[2,8,32,192]{3,2,1,0:T(8,128)(2,1)S(1)}, u32[]{:S(2)}, u32[]{:S(2)}) collective-permute-start(bf16[2,8,32,192]{3,2,1,0:T(8,128)(2,1)} %param.9), channel_id=1, source_target_pairs={{8,0},{16,8},{24,16},{32,24},{40,32},{48,40},{56,48},{64,56},{72,6... | collective-permute-start | bytes 589832 | tf_op jit(solution)/shard_map/ppermute | solution.py:15
  18.9 2.3 collective-permute-done.1
  21.3 3.1 collective-permute-start.2
  24.4 1.3 collective-permute-start.3
  27.0 3.9 collective-permute-done.3
  42.3 1.3 slice.798
  54.9 1.3 slice.786
  57.4 1.3 slice.784
  70.1 1.3 slice.774
  73.9 1.3 slice.771
  75.1 1.3 slice.770
  80.2 1.3 slice.766
  92.8 1.3 slice.754
  100.4 1.3 slice.748
  105.4 1.3 slice.744
  120.2 1.4 concatenate.100
  121.6 1.4 concatenate.99
  122.9 141.4 %all-gather.4.cloned.1.call-done = bf16[5,5,5,192,192]{4,3,2,1,0:T(8,128)(2,1)} async-done(((bf16[5,5,5,24,192]{4,3,2,1,0:T(8,128)(2,1)}), bf16[5,5,5,192,192]{4,3,2,1,0:T(8,128)(2,1)}) %all-gather.4.cloned.1.call-update) | async-done | bytes 9216016 | tf_op jit(solution)/shard_map/all_gather | solution.py:79
  264.4 5.2 %fusion.144 = (bf16[1,5,5,192,192]{4,3,2,1,0:T(8,128)(2,1)S(1)}, bf16[1,5,5,192,192]{4,3,2,1,0:T(8,128)(2,1)S(1)}, bf16[1,5,5,192,192]{4,3,2,1,0:T(8,128)(2,1)S(...) fusion(bf16[5,5,5,192,192]{4,3,2,1,0:T(8,128)(2,1)} %all-gather.4.cloned.1.call-done), kind=kLoop, calls=%fused_computation.222 | loop fusion | bytes 18432000 | tf_op jit(solution)/shard_map/slice | solution.py:40
  272.8 3.0 collective-permute-start.5
  275.8 3.0 collective-permute-start.4
  279.9 1.9 collective-permute-start.6
  281.8 1.3 collective-permute-start.7
  283.1 69.1 %all-gather.6.cloned.1.call-done = bf16[3,3,3,192,192]{4,3,2,1,0:T(8,128)(2,1)} async-done(((bf16[3,3,3,24,192]{4,3,2,1,0:T(8,128)(2,1)}), bf16[3,3,3,192,192]{4,3,2,1,0:T(8,128)(2,1)}) %all-gather.6.cloned.1.call-update) | async-done | bytes 1990672 | tf_op jit(solution)/shard_map/all_gather | solution.py:84
  352.2 1.8 fusion.146
  356.4 3.1 collective-permute-start.9
  359.4 3.0 collective-permute-start.8
  363.5 1.3 collective-permute-start.11
  364.8 4.0 collective-permute-start.10
  368.8 72.6 %all-gather.8.cloned.1.call-done = bf16[3,3,3,192,192]{4,3,2,1,0:T(8,128)(2,1)} async-done(((bf16[3,3,3,24,192]{4,3,2,1,0:T(8,128)(2,1)}), bf16[3,3,3,192,192]{4,3,2,1,0:T(8,128)(2,1)}) %all-gather.8.cloned.1.call-update) | async-done | bytes 1990672 | tf_op jit(solution)/shard_map/all_gather | solution.py:85
  441.4 1.8 fusion.145
  (185 shorter events, 89.1 us)
Async XLA Ops:
  7.2 265.3 %copy-start = (f32[192,192]{1,0:T(8,128)S(1)}, f32[192,192]{1,0:T(8,128)}, u32[]{:S(2)}) copy-start(f32[192,192]{1,0:T(8,128)} %param.13) | copy-start | bytes 442372
  7.2 11.7 %copy-start.2 = (bf16[2,8,32,192]{3,2,1,0:T(8,128)(2,1)S(1)}, bf16[2,8,32,192]{3,2,1,0:T(8,128)(2,1)}, u32[]{:S(2)}) copy-start(bf16[2,8,32,192]{3,2,1,0:T(8,128)(2,1)} %param.9) | copy-start | bytes 589828
  7.2 257.2 %all-gather.4.cloned.1.call-start = ((), (), s32[]{:S(2)}) async-start(), calls=%async_computation | async-start | bytes 13824000 | tf_op jit(solution)/shard_map/all_gather | solution.py:79
  7.9 344.3 %all-gather.6.cloned.1.call-start = ((), (), s32[]{:S(2)}) async-start(), calls=%async_computation.1 | async-start | bytes 2985984 | tf_op jit(solution)/shard_map/all_gather | solution.py:84
  8.7 432.7 %all-gather.8.cloned.1.call-start = ((), (), s32[]{:S(2)}) async-start(), calls=%async_computation.2 | async-start | bytes 2985984 | tf_op jit(solution)/shard_map/all_gather | solution.py:85
  8.7 10.1 %collective-permute-start = (bf16[2,8,32,192]{3,2,1,0:T(8,128)(2,1)}, bf16[2,8,32,192]{3,2,1,0:T(8,128)(2,1)S(1)}, u32[]{:S(2)}, u32[]{:S(2)}) collective-permute-start(bf16[2,8,32,192]{3,2,1,0:T(8,128)(2,1)} %param.9), channel_id=1, source_target_pairs={{0,8},{8,16},{16,24},{24,32},{32,40},{40,48},{48,56},{56,64},{64,7... | collective-permute-start | bytes 589832 | tf_op jit(solution)/shard_map/ppermute | solution.py:14
  13.3 7.9 %collective-permute-start.1 = (bf16[2,8,32,192]{3,2,1,0:T(8,128)(2,1)}, bf16[2,8,32,192]{3,2,1,0:T(8,128)(2,1)S(1)}, u32[]{:S(2)}, u32[]{:S(2)}) collective-permute-start(bf16[2,8,32,192]{3,2,1,0:T(8,128)(2,1)} %param.9), channel_id=1, source_target_pairs={{8,0},{16,8},{24,16},{32,24},{40,32},{48,40},{56,48},{64,56},{72,6... | collective-permute-start | bytes 589832 | tf_op jit(solution)/shard_map/ppermute | solution.py:15
  21.3 5.7 %collective-permute-start.2 = (bf16[6,2,32,192]{3,2,1,0:T(8,128)(2,1)S(1)}, bf16[6,2,32,192]{3,2,1,0:T(8,128)(2,1)S(1)}, u32[]{:S(2)}, u32[]{:S(2)}) collective-permute-start(bf16[6,2,32,192]{3,2,1,0:T(8,128)(2,1)S(1)} %get-tuple-element.30), channel_id=1, source_target_pairs={{0,1},{1,2},{2,3},{3,4},{4,5},{5,6},{6,7},{8,9},{9,10},{10,11},{11... | collective-permute-start | bytes 442376 | tf_op jit(solution)/shard_map/ppermute | solution.py:14
  24.4 6.5 %collective-permute-start.3 = (bf16[6,2,32,192]{3,2,1,0:T(8,128)(2,1)S(1)}, bf16[6,2,32,192]{3,2,1,0:T(8,128)(2,1)S(1)}, u32[]{:S(2)}, u32[]{:S(2)}) collective-permute-start(bf16[6,2,32,192]{3,2,1,0:T(8,128)(2,1)S(1)} %get-tuple-element.31), channel_id=1, source_target_pairs={{1,0},{2,1},{3,2},{4,3},{5,4},{6,5},{7,6},{9,8},{10,9},{11,10},{12... | collective-permute-start | bytes 442376 | tf_op jit(solution)/shard_map/ppermute | solution.py:15
  271.2 0.7 copy-start.3
  271.9 0.7 copy-start.4
  272.8 81.2 %copy-start.1 = (bf16[1,4,16,192]{3,2,1,0:T(8,128)(2,1)}, bf16[1,4,16,192]{3,2,1,0:T(8,128)(2,1)S(1)}, u32[]{:S(2)}) copy-start(bf16[1,4,16,192]{3,2,1,0:T(8,128)(2,1)S(1)} %fusion.14) | copy-start | bytes 73732
  272.8 6.0 %collective-permute-start.5 = (bf16[1,4,16,192]{3,2,1,0:T(8,128)(2,1)S(1)}, bf16[1,4,16,192]{3,2,1,0:T(8,128)(2,1)S(1)}, u32[]{:S(2)}, u32[]{:S(2)}) collective-permute-start(bf16[1,4,16,192]{3,2,1,0:T(8,128)(2,1)S(1)} %fusion.14), channel_id=1, source_target_pairs={{8,0},{16,8},{24,16},{32,24},{40,32},{48,40},{56,48},{64,56},{72,6... | collective-permute-start | bytes 73736 | tf_op jit(solution)/shard_map/ppermute | solution.py:15
  275.8 4.0 collective-permute-start.4
  279.9 74.2 %collective-permute-start.6 = (bf16[3,1,16,192]{3,2,1,0:T(8,128)(2,1)S(1)}, bf16[3,1,16,192]{3,2,1,0:T(8,128)(2,1)S(1)}, u32[]{:S(2)}, u32[]{:S(2)}) collective-permute-start(bf16[3,1,16,192]{3,2,1,0:T(8,128)(2,1)S(1)} %get-tuple-element.79), channel_id=1, source_target_pairs={{0,1},{1,2},{2,3},{3,4},{4,5},{5,6},{6,7},{8,9},{9,10},{10,11},{11... | collective-permute-start | bytes 55304 | tf_op jit(solution)/shard_map/ppermute | solution.py:14
  281.8 72.2 %collective-permute-start.7 = (bf16[3,1,16,192]{3,2,1,0:T(8,128)(2,1)S(1)}, bf16[3,1,16,192]{3,2,1,0:T(8,128)(2,1)S(1)}, u32[]{:S(2)}, u32[]{:S(2)}) collective-permute-start(bf16[3,1,16,192]{3,2,1,0:T(8,128)(2,1)S(1)} %get-tuple-element.80), channel_id=1, source_target_pairs={{1,0},{2,1},{3,2},{4,3},{5,4},{6,5},{7,6},{9,8},{10,9},{11,10},{12... | collective-permute-start | bytes 55304 | tf_op jit(solution)/shard_map/ppermute | solution.py:15
  354.2 2.0 copy-start.5
  356.4 6.1 %collective-permute-start.9 = (bf16[1,4,16,192]{3,2,1,0:T(8,128)(2,1)S(1)}, bf16[1,4,16,192]{3,2,1,0:T(8,128)(2,1)S(1)}, u32[]{:S(2)}, u32[]{:S(2)}) collective-permute-start(bf16[1,4,16,192]{3,2,1,0:T(8,128)(2,1)S(1)} %fusion.15), channel_id=1, source_target_pairs={{8,0},{16,8},{24,16},{32,24},{40,32},{48,40},{56,48},{64,56},{72,6... | collective-permute-start | bytes 73736 | tf_op jit(solution)/shard_map/ppermute | solution.py:15
  359.4 4.0 collective-permute-start.8
  363.5 79.8 %collective-permute-start.11 = (bf16[3,1,16,192]{3,2,1,0:T(8,128)(2,1)S(1)}, bf16[3,1,16,192]{3,2,1,0:T(8,128)(2,1)S(1)}, u32[]{:S(2)}, u32[]{:S(2)}) collective-permute-start(bf16[3,1,16,192]{3,2,1,0:T(8,128)(2,1)S(1)} %get-tuple-element.77), channel_id=1, source_target_pairs={{1,0},{2,1},{3,2},{4,3},{5,4},{6,5},{7,6},{9,8},{10,9},{11,10},{12... | collective-permute-start | bytes 55304 | tf_op jit(solution)/shard_map/ppermute | solution.py:15
  364.8 78.5 %collective-permute-start.10 = (bf16[3,1,16,192]{3,2,1,0:T(8,128)(2,1)S(1)}, bf16[3,1,16,192]{3,2,1,0:T(8,128)(2,1)S(1)}, u32[]{:S(2)}, u32[]{:S(2)}) collective-permute-start(bf16[3,1,16,192]{3,2,1,0:T(8,128)(2,1)S(1)} %get-tuple-element.78), channel_id=1, source_target_pairs={{0,1},{1,2},{2,3},{3,4},{4,5},{5,6},{6,7},{8,9},{9,10},{10,11},{11... | collective-permute-start | bytes 55304 | tf_op jit(solution)/shard_map/ppermute | solution.py:14
  443.4 1.9 copy-start.6
Sparse Core Ops, SparseCore 0:
  11.2 253.1 all-gather.3
  267.6 84.5 all-gather.5
  355.4 85.9 all-gather.7
where the time goes:
time: 453 us
  waiting for transfers between devices  294 us (65%)
  local copies, waits for them, and re-layouts  100 us (22%)
  starting transfers between devices  35.2 us (8%)
  between operations  14.9 us (3%)
  matrix products  7.68 us (2%)
    all_gather x1, waiting for transfers between devices, on_device(): lax.all_gather(analysis_weight, 'narrow', axis=3, tiled=True)  141 us
    slice x125, local copies, waits for them, and re-layouts, strided_conv(): plane[:, second:second + 2 * out_rows - 1:2, third:third + 2 * out_cols -...  85.8 us
    all_gather x1, waiting for transfers between devices, on_device(): lax.all_gather(synthesis_weight, 'narrow', axis=3, tiled=True)  72.6 us
    all_gather x1, waiting for transfers between devices, on_device(): lax.all_gather(hyper_weight, 'narrow', axis=3, tiled=True)  69.1 us
    ppermute x6, starting transfers between devices, padded_2(): before = lax.ppermute(last, axis, up)  19.6 us
    ppermute x6, starting transfers between devices, padded_2(): after = lax.ppermute(leading, axis, down)  15.5 us
  transfers between devices with their start and end apart: 15, of which 8 were waited for; matrix products, arithmetic and copies ran while one was open for 23% of the time, Pallas kernels for 0%

commit v1 on v0

v1 whole, which is shorter than its diff:
```python
import jax
import jax.numpy as jnp
from jax import lax
from jax.experimental import pallas as pl
from jax.experimental.pallas import tpu as pltpu
from jax.sharding import PartitionSpec as P

MESH = pl.DeviceIdType.MESH
F32 = jnp.float32
BF16 = jnp.bfloat16

FAR = ((1, 2), (1, 1), (1, 3), (1, 0))
NEAR = ((0, 2), (0, 1), (0, 3))
TAPS = tuple((a, b, c) for a in range(3) for b in range(3) for c in range(3))


def iota(shape, dim):
    return lax.broadcasted_iota(jnp.int32, shape, dim)


def rows_shifted(x, by):
    n = x.shape[0]
    col = iota(x.shape, 0) & 15
    if by == -1:
        return jnp.where(col == 0, 0.0, pltpu.roll(x, 1, 0))
    return jnp.where(col == 15, 0.0, pltpu.roll(x, n - 1, 0))


def kernel(
    x_ref, w1_ref, b1_ref, beta_ref, gamma_ref, w2_ref, b2_ref, w3_ref, b3_ref,
    lat_ref, sc_ref,
    send1, recv1, from_lo, from_hi, planes, w1k, acc, send2, recv2, wts,
    lat_p, lat_q, hid_p, hid_q,
    s1_send, s1_recv, f_send, f_recv, s2_send, s2_recv,
    g_send, g_recv, c_send, c_recv, l_send, l_recv, h_send, h_recv,
):
    w, n = lax.axis_index("wide"), lax.axis_index("narrow")
    wide = lax.axis_size("wide")
    zh, xx, core = n // 4, n % 4, w % 2
    has_lo, has_hi = w > 0, w < wide - 1
    lo, hi = jnp.maximum(w - 1, 0), jnp.minimum(w + 1, wide - 1)
    sibling = w + 1 - 2 * core

    def peer(e, d):
        return ((zh + e) % 2) * 4 + (xx + d) % 4

    sent = []

    def send(src, dst, ssem, rsem, device, when=None):
        copy = pltpu.make_async_remote_copy(
            src_ref=src, dst_ref=dst, send_sem=ssem, recv_sem=rsem,
            device_id=device, device_id_type=MESH,
        )
        if when is None:
            copy.start()
        else:
            pl.when(when)(copy.start)
        sent.append((copy, when))

    def arrived(dst, rsem, when=None):
        copy = pltpu.make_async_remote_copy(
            src_ref=dst, dst_ref=dst, send_sem=rsem, recv_sem=rsem,
            device_id=(sibling, n), device_id_type=MESH,
        )
        if when is None:
            copy.wait_recv()
        else:
            pl.when(when)(copy.wait_recv)

    barrier = pltpu.get_barrier_semaphore()
    for e, d in FAR + NEAR:
        pl.semaphore_signal(barrier, inc=1, device_id=(w, peer(e, d)), device_id_type=MESH)

    @pl.when(has_lo)
    def _():
        pl.semaphore_signal(barrier, inc=1, device_id=(lo, n), device_id_type=MESH)

    @pl.when(has_hi)
    def _():
        pl.semaphore_signal(barrier, inc=1, device_id=(hi, n), device_id_type=MESH)

    i, j = iota((256, 256), 0), iota((256, 256), 1)
    source = ((i >> 4) & 3) * 64 + (i >> 7) * 32 + (i & 15) * 2 + ((i >> 6) & 1)
    perm = jnp.where(j == source, 1.0, 0.0).astype(BF16)
    cut = [
        jnp.dot(perm, x_ref[256 * z : 256 * z + 256, :], preferred_element_type=F32).astype(BF16)
        for z in range(2)
    ]
    parts = [
        jnp.concatenate([cut[z][64 * t : 64 * t + 64] for z in range(2)], axis=0) for t in range(4)
    ]
    k, l = iota((192, 256), 0), iota((192, 256), 1)
    lane, which = l & 127, l >> 7
    for pair in range(4):
        total = jnp.zeros((128, 256), F32)
        for t in range(4):
            inside = (lane >= 24 * t) & (lane < 24 * t + 24)
            pick = inside & (k == 24 * (2 * pair + which) + lane - 24 * t)
            pick = jnp.where(pick, 1.0, 0.0).astype(BF16)
            total = total + jnp.dot(parts[t], pick, preferred_element_type=F32)
        total = total.astype(BF16)
        for side in range(2):
            for z in range(2):
                send1[2 * pair + side, z] = total[64 * z : 64 * z + 64, 128 * side : 128 * side + 128]

    own_rows = pl.ds(pl.multiple_of(32 * n, 32), 32)
    for layer, ref in ((0, w2_ref), (1, w3_ref)):

        @pl.loop(0, 7)
        def _(t, layer=layer, ref=ref):
            tap = 14 * core + 2 * t
            blank = jnp.zeros((8, 192), F32)
            even = ref[tap].astype(F32)
            odd = ref[jnp.minimum(tap + 1, 26)].astype(F32)
            odd = jnp.where(tap + 1 < 27, odd, 0.0)
            even = jnp.concatenate([even, blank], axis=0)
            odd = jnp.concatenate([odd, blank], axis=0)
            at = 21 * core + 3 * t
            wts[layer, at, own_rows, :] = even[:, :128].astype(BF16)
            wts[layer, at + 1, own_rows, :] = odd[:, :128].astype(BF16)
            both = jnp.concatenate([even[:, 128:], odd[:, 128:]], axis=1)
            wts[layer, at + 2, own_rows, :] = both.astype(BF16)

    pl.semaphore_wait(barrier, 7 + has_lo.astype(jnp.int32) + has_hi.astype(jnp.int32))

    for e, d in FAR + NEAR:
        m = peer(e, d)
        send(send1.at[m], recv1.at[n], s1_send.at[m], s1_recv.at[n], (w, m))
    recv1[n] = send1[n]

    half = pl.ds(21 * core, 21)

    def slice_of(layer, m):
        return wts.at[layer, half, pl.ds(pl.multiple_of(32 * m, 32), 32), :]

    mirror = peer(1, 0)
    for layer in range(2):
        for at, (e, d) in enumerate(((1, 0),) + NEAR):
            m = peer(e, d)
            part = slice_of(layer, n)
            send(part, part, g_send.at[layer, at], g_recv.at[layer, n], (w, m))

    w1k[...] = jnp.zeros_like(w1k)

    @pl.loop(0, 5)
    def _(a):
        for b in range(5):
            step, rp = b // 2, b % 2
            at = a * 3 + step
            v = w1_ref[a * 5 + b].astype(F32)
            last = jnp.concatenate([v[96:120], jnp.zeros((8, 192), F32)], axis=0)
            w1k[at, 48 * rp : 48 * rp + 48, 0:192] = v[0:48].astype(BF16)
            w1k[at, 128 + 48 * rp : 176 + 48 * rp, 0:192] = v[48:96].astype(BF16)
            w1k[at, 96 + 128 * rp : 128 + 128 * rp, 0:192] = last.astype(BF16)

    planes[:, 0:16, :] = jnp.zeros((5, 16, 256), BF16)
    planes[:, 528:544, :] = jnp.zeros((5, 16, 256), BF16)
    acc[0:32, :] = jnp.zeros((32, 256), F32)
    acc[544:576, :] = jnp.zeros((32, 256), F32)

    for turn in range(2):
        for e, d in NEAR if turn == 0 else FAR:
            m = peer(e, d)
            arrived(recv1.at[m], s1_recv.at[m])
        g = (zh + turn) % 2
        four = pl.ds(4 * g, 4)
        send(recv1.at[four], from_lo.at[four], f_send.at[0, turn], f_recv.at[0, g], (hi, n), has_hi)
        send(
            recv1.at[four, 0], from_hi.at[four], f_send.at[1, turn], f_recv.at[1, g], (lo, n), has_lo
        )

    def build(a, read):
        @pl.loop(0, 8)
        def _(blk):
            x = read(blk).astype(F32)
            ln = iota(x.shape, 1)
            after = rows_shifted(x, 1)
            before = jnp.where(ln < 96, rows_shifted(x, -1), pltpu.roll(after, 96, 1))
            same = jnp.where(ln < 96, x, pltpu.roll(after, 48, 1))
            at = pl.ds(pl.multiple_of(16 + 64 * blk, 16), 64)
            planes[a, at, 0:128] = before.astype(BF16)
            planes[a, at, 128:256] = same.astype(BF16)

    def product(a):
        rows = jnp.concatenate([planes[a, 16 * s : 16 * s + 512, :] for s in range(3)], axis=1)
        return jnp.dot(
            rows, w1k[3 * a : 3 * a + 3].reshape(768, 256), preferred_element_type=F32
        )

    build(2, lambda blk: recv1[blk, 0])
    build(3, lambda blk: recv1[blk, 1])
    acc[32:544, :] = product(2)
    acc[32:544, :] += product(3)

    def forward(layer):
        part = slice_of(layer, mirror)
        arrived(part, g_recv.at[layer, mirror])
        for at, (e, d) in enumerate(NEAR):
            send(part, part, g_send.at[layer, 4 + at], g_recv.at[layer, mirror], (w, peer(e, d)))

    def to_sibling(layer):
        for e, d in NEAR + FAR[:3]:
            m = peer(e, d)
            arrived(slice_of(layer, m), g_recv.at[layer, m])
        part = wts.at[layer, half]
        send(part, part, c_send.at[layer], c_recv.at[layer], (sibling, n))

    forward(0)

    @pl.when(jnp.logical_not(has_lo))
    def _():
        from_lo[...] = jnp.zeros_like(from_lo)

    @pl.when(jnp.logical_not(has_hi))
    def _():
        from_hi[...] = jnp.zeros_like(from_hi)

    for g in range(2):
        arrived(from_lo.at[4 * g : 4 * g + 4], f_recv.at[0, g], has_lo)
        arrived(from_hi.at[4 * g : 4 * g + 4], f_recv.at[1, g], has_hi)
    build(0, lambda blk: from_lo[blk, 0])
    build(1, lambda blk: from_lo[blk, 1])
    build(4, lambda blk: from_hi[blk])
    acc[32:544, :] += product(0)
    acc[32:544, :] += product(1)
    acc[32:544, :] += product(4)

    def packed(at):
        rows = acc[at, :]
        left, right = rows[:, :128], rows[:, 128:]
        ln = iota((64, 128), 1)
        side = jnp.where(ln < 64, right[:64], pltpu.roll(right[64:], 64, 1))
        return jnp.concatenate([left, side], axis=0)

    @pl.loop(0, 8)
    def _(m):
        send2[m] = packed(pl.ds(pl.multiple_of(64 * m, 64), 128)).astype(BF16)

    for e, d in FAR + NEAR:
        m = peer(e, d)
        send(send2.at[m], recv2.at[n], s2_send.at[m], s2_recv.at[n], (w, m))
    forward(1)
    to_sibling(0)

    total = packed(pl.ds(pl.multiple_of(64 * n, 64), 128))
    for e, d in NEAR + FAR:
        m = peer(e, d)
        arrived(recv2.at[m], s2_recv.at[m])
        total = total + recv2[m].astype(F32)
    side = total[128:192]
    side = jnp.concatenate([side, pltpu.roll(side, 64, 1)], axis=0)
    conv = jnp.concatenate([total[:128], side[:, :64]], axis=1) + b1_ref[...]
    denom = beta_ref[...] + jnp.dot(
        conv * conv, gamma_ref[...], precision=lax.Precision.HIGHEST, preferred_element_type=F32
    )
    latent = (conv * lax.rsqrt(denom)).astype(BF16)
    lat_ref[...] = latent[32:96]

    k, l = iota((192, 256), 0), iota((192, 256), 1)
    spread = ((l & 31) < 24) & (k == 24 * (l >> 5) + (l & 31))
    spread = jnp.where(spread, 1.0, 0.0).astype(BF16)

    def spread_out(values, first):
        row = first + (iota((values.shape[0], 256), 0) >> 4)
        out = jnp.dot(values.astype(BF16), spread, preferred_element_type=F32)
        return jnp.where((row >= 0) & (row < 32), out, 0.0).astype(BF16)

    def exchange(buf, ssem, rsem):
        send(buf.at[1], buf.at[0], ssem.at[0], rsem.at[0], (hi, n), has_hi)
        send(buf.at[1], buf.at[2], ssem.at[1], rsem.at[1], (lo, n), has_lo)

    def layer_of(layer, buf, buf_q, rsem, rows):
        def shifts(z):
            x = buf[z].astype(F32)
            buf_q[z, 0] = rows_shifted(x, -1).astype(BF16)
            buf_q[z, 1] = rows_shifted(x, 1).astype(BF16)

        sums = [jnp.zeros((rows, 256), F32)] * 2

        def taps(z):
            for tap in range(9 * z, 9 * z + 9):
                _, b, c = TAPS[tap]
                at = pl.ds(16 * b, rows)
                left = buf[z, at, :] if c == 1 else buf_q[z, c // 2, at, :]
                kern = jnp.concatenate(
                    [wts[layer, 3 * (tap // 2) + tap % 2], wts[layer, 3 * (tap // 2) + 2]], axis=1
                )
                sums[tap % 2] += jnp.dot(left, kern, preferred_element_type=F32)

        shifts(1)
        taps(1)

        @pl.when(jnp.logical_not(has_lo))
        def _():
            buf[0] = jnp.zeros_like(buf[0])

        @pl.when(jnp.logical_not(has_hi))
        def _():
            buf[2] = jnp.zeros_like(buf[2])

        arrived(buf.at[0], rsem.at[0], has_lo)
        shifts(0)
        taps(0)
        arrived(buf.at[2], rsem.at[1], has_hi)
        shifts(2)
        taps(2)
        even, odd = sums
        side = even[:, 128:] + pltpu.roll(odd[:, 128:], 64, 1)
        return jnp.concatenate([even[:, :128] + odd[:, :128], side[:, :64]], axis=1)

    lat_p[1] = spread_out(jnp.abs(latent), 4 * n - 2)
    exchange(lat_p, l_send, l_recv)
    other = pl.ds(21 * (1 - core), 21)
    arrived(wts.at[0, other], c_recv.at[0])
    to_sibling(1)
    hidden = jnp.maximum(layer_of(0, lat_p, lat_q, l_recv, 96) + b2_ref[...], 0.0)
    hid_p[1] = spread_out(hidden, 4 * n - 1)
    exchange(hid_p, h_send, h_recv)
    arrived(wts.at[1, other], c_recv.at[1])
    s = layer_of(1, hid_p, hid_q, h_recv, 64) + b3_ref[...]
    sc_ref[...] = 0.11 + (jnp.maximum(s, 0.0) + jnp.log1p(jnp.exp(-jnp.abs(s))))

    for copy, when in sent:
        if when is None:
            copy.wait_send()
        else:
            pl.when(when)(copy.wait_send)


def on_device(density, w1, b1, beta, gamma, w2, b2, w3, b3):
    vmem = pl.BlockSpec(memory_space=pltpu.VMEM)
    dma = pltpu.SemaphoreType.DMA
    latent, scales = pl.pallas_call(
        kernel,
        out_shape=(
            jax.ShapeDtypeStruct((64, 192), BF16),
            jax.ShapeDtypeStruct((64, 192), F32),
        ),
        in_specs=[vmem] * 9,
        out_specs=(vmem, vmem),
        scratch_shapes=[
            pltpu.VMEM((8, 2, 64, 128), BF16),
            pltpu.VMEM((8, 2, 64, 128), BF16),
            pltpu.VMEM((8, 2, 64, 128), BF16),
            pltpu.VMEM((8, 64, 128), BF16),
            pltpu.VMEM((5, 544, 256), BF16),
            pltpu.VMEM((15, 256, 256), BF16),
            pltpu.VMEM((576, 256), F32),
            pltpu.VMEM((8, 192, 128), BF16),
            pltpu.VMEM((8, 192, 128), BF16),
            pltpu.VMEM((2, 42, 256, 128), BF16),
            pltpu.VMEM((3, 128, 256), BF16),
            pltpu.VMEM((3, 2, 128, 256), BF16),
            pltpu.VMEM((3, 96, 256), BF16),
            pltpu.VMEM((3, 2, 96, 256), BF16),
            dma((8,)), dma((8,)),
            dma((2, 2)), dma((2, 2)),
            dma((8,)), dma((8,)),
            dma((2, 7)), dma((2, 8)),
            dma((2,)), dma((2,)),
            dma((2,)), dma((2,)),
            dma((2,)), dma((2,)),
        ],
        compiler_params=pltpu.CompilerParams(
            collective_id=0, has_side_effects=True, vmem_limit_bytes=48 * 2**20
        ),
    )(
        density.reshape(512, 192),
        w1.reshape(25, 120, 192),
        b1.reshape(1, 192),
        beta.reshape(1, 192),
        gamma,
        w2.reshape(27, 24, 192),
        b2.reshape(1, 192),
        w3.reshape(27, 24, 192),
        b3.reshape(1, 192),
    )
    return latent.reshape(1, 4, 16, 192), scales.reshape(1, 4, 16, 192)


def solution(mesh):
    in_specs = (
        P("wide", "narrow", None, None),
        P(None, None, None, "narrow", None),
        P(),
        P(),
        P(),
        P(None, None, None, "narrow", None),
        P(),
        P(None, None, None, "narrow", None),
        P(),
    )
    out_specs = (P("wide", "narrow", None, None), P("wide", "narrow", None, None))
    return jax.shard_map(
        on_device, mesh=mesh, in_specs=in_specs, out_specs=out_specs, check_vma=False
    )
```

time: 453 us -> 67.8 us (0.15)
  waiting for transfers between devices: 294 us -> 0 us
  local copies, waits for them, and re-layouts: 100 us -> 9.17 us
  Pallas kernels: 0 us -> 57.3 us
  starting transfers between devices: 35.2 us -> 0 us
  between operations: 14.9 us -> 0.66 us
  matrix products: 7.68 us -> 0 us
    all_gather x3 -> x0, waiting for transfers between devices: 283 us -> none  [the longest x1 141 us: on_device(): lax.all_gather(analysis_weight, 'narrow', axis=3, tiled=True)]
    slice x133 -> x0, local copies, waits for them, and re-layouts: 95 us -> none  [the longest x125 85.8 us: strided_conv(): plane[:, second:second + 2 * out_rows - 1:2, third:third + 2 * out_cols -...]
    pallas_call x0 -> x1, Pallas kernels: none -> 57.3 us  [on_device(): pl.pallas_call(kernel, out_shape=(jax.ShapeDtypeStruct((64, 192), BF16),...]
    ppermute x12 -> x0, starting transfers between devices: 35.1 us -> none  [the longest x6 19.6 us: padded_2(): before = lax.ppermute(last, axis, up)]
    ppermute x12 -> x0, waiting for transfers between devices: 9.48 us -> none  [the longest x6 6.23 us: padded_2(): after = lax.ppermute(leading, axis, down)]
    unnamed x16 -> x20, local copies, waits for them, and re-layouts: 0.3 us -> 9.17 us
    dot_general x24 -> x0, matrix products: 7.68 us -> none  [the longest x18 4.73 us: cube_conv(): total = total + jnp.dot(stacked, kernel, preferred_element_type=jnp.float32)]
    concatenate x6 -> x0, local copies, waits for them, and re-layouts: 4.82 us -> none  [the longest x5 4.8 us: strided_conv(): jnp.concatenate([plane[:, second:second + 2 * out_rows - 1:2, third:third...]
  transfers between devices with their start and end apart: 15 -> 0, of which waited for: 8 -> 0; matrix products, arithmetic and copies ran while one was open for 23% -> 0% of each run, Pallas kernels for 0% -> 0%
where the time goes in v1:
time: 67.8 us; the launch traced here: 67.1 us
  Pallas kernels  57.3 us (85%)
  local copies, waits for them, and re-layouts  9.17 us (14%)
    pallas_call x1, Pallas kernels, on_device(): pl.pallas_call(kernel, out_shape=(jax.ShapeDtypeStruct((64, 192), BF16),...  57.3 us
    unnamed x20, local copies, waits for them, and re-layouts  9.17 us

profile of v1, /device:TPU:1, one launch (start us, length us, event | category | flops | bytes accessed | tf_op | source)
XLA Modules:
  0.0 67.1 jit_solution(7137805191284299204)
XLA Ops:
  0.6 0.0 copy-start
  0.6 1.4 %copy-done = bf16[5,5,5,24,192]{4,3,2,1,0:T(8,128)(2,1)S(1)} copy-done((bf16[5,5,5,24,192]{4,3,2,1,0:T(8,128)(2,1)S(1)}, bf16[5,5,5,24,192]{4,3,2,1,0:T(8,128)(2,1)}, u32[]{:S(2)}) %copy-start) | copy-done | bytes 1152024
  2.0 0.0 copy-start.1
  2.0 1.0 %copy-done.1 = bf16[3,3,3,24,192]{4,3,2,1,0:T(8,128)(2,1)S(1)} copy-done((bf16[3,3,3,24,192]{4,3,2,1,0:T(8,128)(2,1)S(1)}, bf16[3,3,3,24,192]{4,3,2,1,0:T(8,128)(2,1)}, u32[]{:S(2)}) %copy-start.1) | copy-done | bytes 248856
  3.0 0.0 copy-start.2
  3.0 1.0 %copy-done.2 = bf16[3,3,3,24,192]{4,3,2,1,0:T(8,128)(2,1)S(1)} copy-done((bf16[3,3,3,24,192]{4,3,2,1,0:T(8,128)(2,1)S(1)}, bf16[3,3,3,24,192]{4,3,2,1,0:T(8,128)(2,1)}, u32[]{:S(2)}) %copy-start.2) | copy-done | bytes 248856
  4.0 0.0 copy-start.3
  4.0 0.9 %copy-done.3 = bf16[2,8,32,192]{3,2,1,0:T(8,128)(2,1)S(1)} copy-done((bf16[2,8,32,192]{3,2,1,0:T(8,128)(2,1)S(1)}, bf16[2,8,32,192]{3,2,1,0:T(8,128)(2,1)}, u32[]{:S(2)}) %copy-start.3) | copy-done | bytes 196632
  4.9 0.0 copy-start.4
  4.9 0.9 %copy-done.4 = f32[192,192]{1,0:T(8,128)S(1)} copy-done((f32[192,192]{1,0:T(8,128)S(1)}, f32[192,192]{1,0:T(8,128)}, u32[]{:S(2)}) %copy-start.4) | copy-done | bytes 147480
  5.9 0.0 copy-start.5
  5.9 0.7 %copy-done.5 = f32[192]{0:T(256)S(1)} copy-done((f32[192]{0:T(256)S(1)}, f32[192]{0:T(256)}, u32[]{:S(2)}) %copy-start.5) | copy-done | bytes 792
  6.5 0.0 copy-start.6
  6.5 0.7 %copy-done.6 = f32[192]{0:T(256)S(1)} copy-done((f32[192]{0:T(256)S(1)}, f32[192]{0:T(256)}, u32[]{:S(2)}) %copy-start.6) | copy-done | bytes 792
  7.2 0.0 copy-start.7
  7.2 0.7 %copy-done.7 = f32[192]{0:T(256)S(1)} copy-done((f32[192]{0:T(256)S(1)}, f32[192]{0:T(256)}, u32[]{:S(2)}) %copy-start.7) | copy-done | bytes 792
  7.9 0.0 copy-start.8
  7.9 0.7 %copy-done.8 = f32[192]{0:T(256)S(1)} copy-done((f32[192]{0:T(256)S(1)}, f32[192]{0:T(256)}, u32[]{:S(2)}) %copy-start.8) | copy-done | bytes 792
  8.6 57.3 %shard_map.104 = (bf16[64,192]{1,0:T(8,128)(2,1)S(1)}, f32[64,192]{1,0:T(8,128)S(1)}) custom-call(bf16[512,192]{1,0:T(8,128)(2,1)S(1)} %bitcast.13, bf16[25,120,192]{2,1,0:T(8,128)(2,1)S(1)} %bitcast.10, f32[1,192]{1,0:T(1,128)S(1)} %bitcast.16, f32[1,192]{1,0:T(1,128)S(1)} %bitcast.17, f32[192,192]{1,0:T(8,128)S(1)} %copy-done.4, ...), custom_call_target="tpu_custom_call" | custom-call | tf_op jit(solution)/shard_map/pallas_call | solution.py:333
  65.9 0.6 copy.13
  66.5 0.6 copy.14
Async XLA Ops:
  0.6 1.4 %copy-start = (bf16[5,5,5,24,192]{4,3,2,1,0:T(8,128)(2,1)S(1)}, bf16[5,5,5,24,192]{4,3,2,1,0:T(8,128)(2,1)}, u32[]{:S(2)}) copy-start(bf16[5,5,5,24,192]{4,3,2,1,0:T(8,128)(2,1)} %param.10) | copy-start | bytes 3456004
  2.0 1.0 %copy-start.1 = (bf16[3,3,3,24,192]{4,3,2,1,0:T(8,128)(2,1)S(1)}, bf16[3,3,3,24,192]{4,3,2,1,0:T(8,128)(2,1)}, u32[]{:S(2)}) copy-start(bf16[3,3,3,24,192]{4,3,2,1,0:T(8,128)(2,1)} %param.14) | copy-start | bytes 746500
  3.0 1.0 %copy-start.2 = (bf16[3,3,3,24,192]{4,3,2,1,0:T(8,128)(2,1)S(1)}, bf16[3,3,3,24,192]{4,3,2,1,0:T(8,128)(2,1)}, u32[]{:S(2)}) copy-start(bf16[3,3,3,24,192]{4,3,2,1,0:T(8,128)(2,1)} %param.16) | copy-start | bytes 746500
  4.0 0.9 %copy-start.3 = (bf16[2,8,32,192]{3,2,1,0:T(8,128)(2,1)S(1)}, bf16[2,8,32,192]{3,2,1,0:T(8,128)(2,1)}, u32[]{:S(2)}) copy-start(bf16[2,8,32,192]{3,2,1,0:T(8,128)(2,1)} %param.9) | copy-start | bytes 589828
  4.9 0.9 %copy-start.4 = (f32[192,192]{1,0:T(8,128)S(1)}, f32[192,192]{1,0:T(8,128)}, u32[]{:S(2)}) copy-start(f32[192,192]{1,0:T(8,128)} %gamma_ref.1) | copy-start | bytes 442372
  5.9 0.7 %copy-start.5 = (f32[192]{0:T(256)S(1)}, f32[192]{0:T(256)}, u32[]{:S(2)}) copy-start(f32[192]{0:T(256)} %param.11) | copy-start | bytes 2308
  6.5 0.7 %copy-start.6 = (f32[192]{0:T(256)S(1)}, f32[192]{0:T(256)}, u32[]{:S(2)}) copy-start(f32[192]{0:T(256)} %param.12) | copy-start | bytes 2308
  7.2 0.7 %copy-start.7 = (f32[192]{0:T(256)S(1)}, f32[192]{0:T(256)}, u32[]{:S(2)}) copy-start(f32[192]{0:T(256)} %param.15) | copy-start | bytes 2308
  7.9 0.7 %copy-start.8 = (f32[192]{0:T(256)S(1)}, f32[192]{0:T(256)}, u32[]{:S(2)}) copy-start(f32[192]{0:T(256)} %param.17) | copy-start | bytes 2308

commit v2 on v1

--- a/solution.py
+++ b/solution.py
@@ -27,13 +27,23 @@
 
 
 def kernel(
-    x_ref, w1_ref, b1_ref, beta_ref, gamma_ref, w2_ref, b2_ref, w3_ref, b3_ref,
+    x_in, w1_in, b1_in, beta_in, gamma_in, w2_in, b2_in, w3_in, b3_in,
     lat_ref, sc_ref,
+    x_ref, w1_ref, b1_ref, beta_ref, gamma_ref, w2_ref, b2_ref, w3_ref, b3_ref, in_sem,
     send1, recv1, from_lo, from_hi, planes, w1k, acc, send2, recv2, wts,
     lat_p, lat_q, hid_p, hid_q,
     s1_send, s1_recv, f_send, f_recv, s2_send, s2_recv,
     g_send, g_recv, c_send, c_recv, l_send, l_recv, h_send, h_recv,
 ):
+    loads = [
+        pltpu.make_async_copy(src, dst, in_sem.at[i])
+        for i, (src, dst) in enumerate((
+            (x_in, x_ref), (w2_in, w2_ref), (w3_in, w3_ref), (w1_in, w1_ref), (gamma_in, gamma_ref),
+            (b1_in, b1_ref), (beta_in, beta_ref), (b2_in, b2_ref), (b3_in, b3_ref),
+        ))
+    ]
+    for load in loads:
+        load.start()
     w, n = lax.axis_index("wide"), lax.axis_index("narrow")
     wide = lax.axis_size("wide")
     zh, xx, core = n // 4, n % 4, w % 2
@@ -79,6 +89,7 @@
     def _():
         pl.semaphore_signal(barrier, inc=1, device_id=(hi, n), device_id_type=MESH)
 
+    loads[0].wait()
     i, j = iota((256, 256), 0), iota((256, 256), 1)
     source = ((i >> 4) & 3) * 64 + (i >> 7) * 32 + (i & 15) * 2 + ((i >> 6) & 1)
     perm = jnp.where(j == source, 1.0, 0.0).astype(BF16)
@@ -103,24 +114,6 @@
             for z in range(2):
                 send1[2 * pair + side, z] = total[64 * z : 64 * z + 64, 128 * side : 128 * side + 128]
 
-    own_rows = pl.ds(pl.multiple_of(32 * n, 32), 32)
-    for layer, ref in ((0, w2_ref), (1, w3_ref)):
-
-        @pl.loop(0, 7)
-        def _(t, layer=layer, ref=ref):
-            tap = 14 * core + 2 * t
-            blank = jnp.zeros((8, 192), F32)
-            even = ref[tap].astype(F32)
-            odd = ref[jnp.minimum(tap + 1, 26)].astype(F32)
-            odd = jnp.where(tap + 1 < 27, odd, 0.0)
-            even = jnp.concatenate([even, blank], axis=0)
-            odd = jnp.concatenate([odd, blank], axis=0)
-            at = 21 * core + 3 * t
-            wts[layer, at, own_rows, :] = even[:, :128].astype(BF16)
-            wts[layer, at + 1, own_rows, :] = odd[:, :128].astype(BF16)
-            both = jnp.concatenate([even[:, 128:], odd[:, 128:]], axis=1)
-            wts[layer, at + 2, own_rows, :] = both.astype(BF16)
-
     pl.semaphore_wait(barrier, 7 + has_lo.astype(jnp.int32) + has_hi.astype(jnp.int32))
 
     for e, d in FAR + NEAR:
@@ -128,17 +121,49 @@
         send(send1.at[m], recv1.at[n], s1_send.at[m], s1_recv.at[n], (w, m))
     recv1[n] = send1[n]
 
+    for load in loads[1:]:
+        load.wait()
+
+    for layer, ref in ((0, w2_ref), (1, w3_ref)):
+
+        @pl.loop(0, 7)
+        def _(t, layer=layer, ref=ref):
+            tap = 14 * core + 2 * t
+            even = ref[tap].astype(F32)
+            odd = ref[jnp.minimum(tap + 1, 26)].astype(F32)
+            odd = jnp.where(tap + 1 < 27, odd, 0.0)
+            at = 21 * core + 3 * t
+            wts[layer, at, n] = even[:, :128].astype(BF16)
+            wts[layer, at + 1, n] = odd[:, :128].astype(BF16)
+            both = jnp.concatenate([even[:, 128:], odd[:, 128:]], axis=1)
+            wts[layer, at + 2, n] = both.astype(BF16)
+
     half = pl.ds(21 * core, 21)
 
     def slice_of(layer, m):
-        return wts.at[layer, half, pl.ds(pl.multiple_of(32 * m, 32), 32), :]
+        return wts.at[layer, half, m]
 
     mirror = peer(1, 0)
-    for layer in range(2):
+
+    def to_peers(layer):
+        part = slice_of(layer, n)
         for at, (e, d) in enumerate(((1, 0),) + NEAR):
+            send(part, part, g_send.at[layer, at], g_recv.at[layer, n], (w, peer(e, d)))
+
+    def forward(layer):
+        part = slice_of(layer, mirror)
+        arrived(part, g_recv.at[layer, mirror])
+        for at, (e, d) in enumerate(NEAR):
+            send(part, part, g_send.at[layer, 4 + at], g_recv.at[layer, mirror], (w, peer(e, d)))
+
+    def to_sibling(layer):
+        for e, d in NEAR + FAR[:3]:
             m = peer(e, d)
-            part = slice_of(layer, n)
-            send(part, part, g_send.at[layer, at], g_recv.at[layer, n], (w, m))
+            arrived(slice_of(layer, m), g_recv.at[layer, m])
+        part = wts.at[layer, half]
+        send(part, part, c_send.at[layer], c_recv.at[layer], (sibling, n))
+
+    to_peers(0)
 
     w1k[...] = jnp.zeros_like(w1k)
 
@@ -168,10 +193,13 @@
         send(
             recv1.at[four, 0], from_hi.at[four], f_send.at[1, turn], f_recv.at[1, g], (lo, n), has_lo
         )
-
-    def build(a, read):
-        @pl.loop(0, 8)
-        def _(blk):
+        if turn == 0:
+            to_peers(1)
+
+    def build(a, read, begin=0, count=8):
+        @pl.loop(0, count)
+        def _(step):
+            blk = begin + step
             x = read(blk).astype(F32)
             ln = iota(x.shape, 1)
             after = rows_shifted(x, 1)
@@ -181,31 +209,17 @@
             planes[a, at, 0:128] = before.astype(BF16)
             planes[a, at, 128:256] = same.astype(BF16)
 
-    def product(a):
-        rows = jnp.concatenate([planes[a, 16 * s : 16 * s + 512, :] for s in range(3)], axis=1)
+    def product(a, first=0, size=512):
+        rows = jnp.concatenate(
+            [planes[a, pl.ds(first + 16 * s, size), :] for s in range(3)], axis=1
+        )
         return jnp.dot(
             rows, w1k[3 * a : 3 * a + 3].reshape(768, 256), preferred_element_type=F32
         )
 
     build(2, lambda blk: recv1[blk, 0])
     build(3, lambda blk: recv1[blk, 1])
-    acc[32:544, :] = product(2)
-    acc[32:544, :] += product(3)
-
-    def forward(layer):
-        part = slice_of(layer, mirror)
-        arrived(part, g_recv.at[layer, mirror])
-        for at, (e, d) in enumerate(NEAR):
-            send(part, part, g_send.at[layer, 4 + at], g_recv.at[layer, mirror], (w, peer(e, d)))
-
-    def to_sibling(layer):
-        for e, d in NEAR + FAR[:3]:
-            m = peer(e, d)
-            arrived(slice_of(layer, m), g_recv.at[layer, m])
-        part = wts.at[layer, half]
-        send(part, part, c_send.at[layer], c_recv.at[layer], (sibling, n))
-
-    forward(0)
+    acc[32:544, :] = product(2) + product(3)
 
     @pl.when(jnp.logical_not(has_lo))
     def _():
@@ -215,15 +229,20 @@
     def _():
         from_hi[...] = jnp.zeros_like(from_hi)
 
-    for g in range(2):
-        arrived(from_lo.at[4 * g : 4 * g + 4], f_recv.at[0, g], has_lo)
-        arrived(from_hi.at[4 * g : 4 * g + 4], f_recv.at[1, g], has_hi)
-    build(0, lambda blk: from_lo[blk, 0])
-    build(1, lambda blk: from_lo[blk, 1])
-    build(4, lambda blk: from_hi[blk])
-    acc[32:544, :] += product(0)
-    acc[32:544, :] += product(1)
-    acc[32:544, :] += product(4)
+    for turn in range(2):
+        g = (zh + turn) % 2
+        four = pl.ds(4 * g, 4)
+        arrived(from_lo.at[four], f_recv.at[0, g], has_lo)
+        arrived(from_hi.at[four], f_recv.at[1, g], has_hi)
+        if turn == 1:
+            forward(0)
+        build(0, lambda blk: from_lo[blk, 0], 4 * g, 4)
+        build(1, lambda blk: from_lo[blk, 1], 4 * g, 4)
+        build(4, lambda blk: from_hi[blk], 4 * g, 4)
+        size = (240, 272)[turn]
+        first = pl.multiple_of(zh * 272 if turn == 0 else (1 - zh) * 240, 16)
+        add = product(0, first, size) + product(1, first, size) + product(4, first, size)
+        acc[pl.ds(pl.multiple_of(32 + first, 16), size), :] += add
 
     def packed(at):
         rows = acc[at, :]
@@ -256,18 +275,16 @@
     latent = (conv * lax.rsqrt(denom)).astype(BF16)
     lat_ref[...] = latent[32:96]
 
-    k, l = iota((192, 256), 0), iota((192, 256), 1)
-    spread = ((l & 31) < 24) & (k == 24 * (l >> 5) + (l & 31))
-    spread = jnp.where(spread, 1.0, 0.0).astype(BF16)
-
-    def spread_out(values, first):
-        row = first + (iota((values.shape[0], 256), 0) >> 4)
-        out = jnp.dot(values.astype(BF16), spread, preferred_element_type=F32)
-        return jnp.where((row >= 0) & (row < 32), out, 0.0).astype(BF16)
+    def inside(values, first):
+        row = first + (iota(values.shape, 0) >> 4)
+        return jnp.where((row >= 0) & (row < 32), values, 0.0).astype(BF16)
 
     def exchange(buf, ssem, rsem):
         send(buf.at[1], buf.at[0], ssem.at[0], rsem.at[0], (hi, n), has_hi)
         send(buf.at[1], buf.at[2], ssem.at[1], rsem.at[1], (lo, n), has_lo)
+
+    def kernel_of(layer, at):
+        return wts[layer, at].reshape(192, 128)
 
     def layer_of(layer, buf, buf_q, rsem, rows):
         def shifts(z):
@@ -283,7 +300,8 @@
                 at = pl.ds(16 * b, rows)
                 left = buf[z, at, :] if c == 1 else buf_q[z, c // 2, at, :]
                 kern = jnp.concatenate(
-                    [wts[layer, 3 * (tap // 2) + tap % 2], wts[layer, 3 * (tap // 2) + 2]], axis=1
+                    [kernel_of(layer, 3 * (tap // 2) + tap % 2), kernel_of(layer, 3 * (tap // 2) + 2)],
+                    axis=1,
                 )
                 sums[tap % 2] += jnp.dot(left, kern, preferred_element_type=F32)
 
@@ -308,13 +326,13 @@
         side = even[:, 128:] + pltpu.roll(odd[:, 128:], 64, 1)
         return jnp.concatenate([even[:, :128] + odd[:, :128], side[:, :64]], axis=1)
 
-    lat_p[1] = spread_out(jnp.abs(latent), 4 * n - 2)
+    lat_p[1] = inside(jnp.abs(latent.astype(F32)), 4 * n - 2)
     exchange(lat_p, l_send, l_recv)
     other = pl.ds(21 * (1 - core), 21)
     arrived(wts.at[0, other], c_recv.at[0])
     to_sibling(1)
     hidden = jnp.maximum(layer_of(0, lat_p, lat_q, l_recv, 96) + b2_ref[...], 0.0)
-    hid_p[1] = spread_out(hidden, 4 * n - 1)
+    hid_p[1] = inside(hidden, 4 * n - 1)
     exchange(hid_p, h_send, h_recv)
     arrived(wts.at[1, other], c_recv.at[1])
     s = layer_of(1, hid_p, hid_q, h_recv, 64) + b3_ref[...]
@@ -336,9 +354,19 @@
             jax.ShapeDtypeStruct((64, 192), BF16),
             jax.ShapeDtypeStruct((64, 192), F32),
         ),
-        in_specs=[vmem] * 9,
+        in_specs=[pl.BlockSpec(memory_space=pl.ANY)] * 9,
         out_specs=(vmem, vmem),
         scratch_shapes=[
+            pltpu.VMEM((512, 192), BF16),
+            pltpu.VMEM((25, 120, 192), BF16),
+            pltpu.VMEM((1, 192), F32),
+            pltpu.VMEM((1, 192), F32),
+            pltpu.VMEM((192, 192), F32),
+            pltpu.VMEM((27, 24, 192), BF16),
+            pltpu.VMEM((1, 192), F32),
+            pltpu.VMEM((27, 24, 192), BF16),
+            pltpu.VMEM((1, 192), F32),
+            dma((9,)),
             pltpu.VMEM((8, 2, 64, 128), BF16),
             pltpu.VMEM((8, 2, 64, 128), BF16),
             pltpu.VMEM((8, 2, 64, 128), BF16),
@@ -348,11 +376,11 @@
             pltpu.VMEM((576, 256), F32),
             pltpu.VMEM((8, 192, 128), BF16),
             pltpu.VMEM((8, 192, 128), BF16),
-            pltpu.VMEM((2, 42, 256, 128), BF16),
-            pltpu.VMEM((3, 128, 256), BF16),
-            pltpu.VMEM((3, 2, 128, 256), BF16),
-            pltpu.VMEM((3, 96, 256), BF16),
-            pltpu.VMEM((3, 2, 96, 256), BF16),
+            pltpu.VMEM((2, 42, 8, 24, 128), BF16),
+            pltpu.VMEM((3, 128, 192), BF16),
+            pltpu.VMEM((3, 2, 128, 192), BF16),
+            pltpu.VMEM((3, 96, 192), BF16),
+            pltpu.VMEM((3, 2, 96, 192), BF16),
             dma((8,)), dma((8,)),
             dma((2, 2)), dma((2, 2)),
             dma((8,)), dma((8,)),
@@ -362,7 +390,7 @@
             dma((2,)), dma((2,)),
         ],
         compiler_params=pltpu.CompilerParams(
-            collective_id=0, has_side_effects=True, vmem_limit_bytes=48 * 2**20
+            collective_id=0, has_side_effects=True, vmem_limit_bytes=60 * 2**20
         ),
     )(
         density.reshape(512, 192),

time: 67.8 us -> 56.8 us (0.84)
  the two profiles are of different devices: /device:TPU:1 before, /device:TPU:121 now
where the time goes in v2:
time: 56.8 us; the launch traced here: 56.5 us
  Pallas kernels  53 us (93%)
  local copies, waits for them, and re-layouts  2.85 us (5%)
  between operations  0.64 us (1%)
    pallas_call x1, Pallas kernels, on_device(): pl.pallas_call(kernel, out_shape=(jax.ShapeDtypeStruct((64, 192), BF16),...  53 us
    unnamed x2, local copies, waits for them, and re-layouts  2.85 us

profile of v2, /device:TPU:121, one launch (start us, length us, event | category | flops | bytes accessed | tf_op | source)
XLA Modules:
  0.0 56.5 jit_solution(15101098334533357221)
XLA Ops:
  0.6 53.0 %shard_map.104 = (bf16[64,192]{1,0:T(8,128)(2,1)}, f32[64,192]{1,0:T(8,128)}) custom-call(bf16[512,192]{1,0:T(8,128)(2,1)} %bitcast.13, bf16[25,120,192]{2,1,0:T(8,128)(2,1)} %bitcast.10, f32[1,192]{1,0:T(1,128)} %bitcast.16, f32[1,192]{1,0:T(1,128)} %bitcast.17, f32[192,192]{1,0:T(8,128)} %gamma_in.1, bf16[27,24,192]{2,1,0:T(8,128)(2,1)} %bitcast.11, ...), custom_call_target="tpu_custom_call" | custom-call | tf_op jit(solution)/shard_map/pallas_call | solution.py:351
  53.7 1.4 %copy.13 = bf16[1,4,16,192]{3,2,1,0:T(8,128)(2,1)} copy(bf16[1,4,16,192]{3,2,1,0:T(8,128)(2,1)} %bitcast.15) | data formatting | bytes 49152
  55.0 1.5 %copy.14 = f32[1,4,16,192]{3,2,1,0:T(8,128)} copy(f32[1,4,16,192]{3,2,1,0:T(8,128)} %bitcast.14) | data formatting | bytes 98304

commit v3 on v2

--- a/solution.py
+++ b/solution.py
@@ -33,7 +33,7 @@
     send1, recv1, from_lo, from_hi, planes, w1k, acc, send2, recv2, wts,
     lat_p, lat_q, hid_p, hid_q,
     s1_send, s1_recv, f_send, f_recv, s2_send, s2_recv,
-    g_send, g_recv, c_send, c_recv, l_send, l_recv, h_send, h_recv,
+    g_send, g_recv, y_send, y_recv, c_send, c_recv, l_send, l_recv, h_send, h_recv,
 ):
     loads = [
         pltpu.make_async_copy(src, dst, in_sem.at[i])
@@ -47,6 +47,9 @@
     w, n = lax.axis_index("wide"), lax.axis_index("narrow")
     wide = lax.axis_size("wide")
     zh, xx, core = n // 4, n % 4, w % 2
+    yy = (w // 2) % 8
+    y_up, y_down = w + 2 * ((yy + 1) % 8 - yy), w + 2 * ((yy + 7) % 8 - yy)
+    quarter = 2 * core + yy % 2
     has_lo, has_hi = w > 0, w < wide - 1
     lo, hi = jnp.maximum(w - 1, 0), jnp.minimum(w + 1, wide - 1)
     sibling = w + 1 - 2 * core
@@ -80,6 +83,9 @@
     barrier = pltpu.get_barrier_semaphore()
     for e, d in FAR + NEAR:
         pl.semaphore_signal(barrier, inc=1, device_id=(w, peer(e, d)), device_id_type=MESH)
+
+    for y in (y_up, y_down):
+        pl.semaphore_signal(barrier, inc=1, device_id=(y, n), device_id_type=MESH)
 
     @pl.when(has_lo)
     def _():
@@ -109,12 +115,15 @@
             pick = inside & (k == 24 * (2 * pair + which) + lane - 24 * t)
             pick = jnp.where(pick, 1.0, 0.0).astype(BF16)
             total = total + jnp.dot(parts[t], pick, preferred_element_type=F32)
-        total = total.astype(BF16)
         for side in range(2):
-            for z in range(2):
-                send1[2 * pair + side, z] = total[64 * z : 64 * z + 64, 128 * side : 128 * side + 128]
-
-    pl.semaphore_wait(barrier, 7 + has_lo.astype(jnp.int32) + has_hi.astype(jnp.int32))
+            first = total[:64, 128 * side : 128 * side + 128]
+            second = pltpu.roll(total[64:, 128 * side : 128 * side + 128], 96, 1)
+            ln = iota((64, 128), 1)
+            rest = jnp.where(ln[:32] < 64, second[:32], pltpu.roll(second[32:], 64, 1))
+            block = jnp.concatenate([jnp.where(ln < 96, first, second), rest], axis=0)
+            send1[2 * pair + side] = block.astype(BF16)
+
+    pl.semaphore_wait(barrier, 9 + has_lo.astype(jnp.int32) + has_hi.astype(jnp.int32))
 
     for e, d in FAR + NEAR:
         m = peer(e, d)
@@ -126,24 +135,21 @@
 
     for layer, ref in ((0, w2_ref), (1, w3_ref)):
 
-        @pl.loop(0, 7)
+        @pl.loop(0, 11)
         def _(t, layer=layer, ref=ref):
-            tap = 14 * core + 2 * t
-            even = ref[tap].astype(F32)
+            at = 11 * quarter + t
+            tap, kind = 2 * (at // 3), at % 3
+            even = ref[jnp.minimum(tap, 26)].astype(F32)
             odd = ref[jnp.minimum(tap + 1, 26)].astype(F32)
             odd = jnp.where(tap + 1 < 27, odd, 0.0)
-            at = 21 * core + 3 * t
-            wts[layer, at, n] = even[:, :128].astype(BF16)
-            wts[layer, at + 1, n] = odd[:, :128].astype(BF16)
             both = jnp.concatenate([even[:, 128:], odd[:, 128:]], axis=1)
-            wts[layer, at + 2, n] = both.astype(BF16)
-
-    half = pl.ds(21 * core, 21)
+            value = jnp.where(kind == 0, even[:, :128], jnp.where(kind == 1, odd[:, :128], both))
+            wts[layer, at, n] = value.astype(BF16)
+
+    mirror = peer(1, 0)
 
     def slice_of(layer, m):
-        return wts.at[layer, half, m]
-
-    mirror = peer(1, 0)
+        return wts.at[layer, pl.ds(11 * quarter, 11), m]
 
     def to_peers(layer):
         part = slice_of(layer, n)
@@ -156,27 +162,55 @@
         for at, (e, d) in enumerate(NEAR):
             send(part, part, g_send.at[layer, 4 + at], g_recv.at[layer, mirror], (w, peer(e, d)))
 
-    def to_sibling(layer):
-        for e, d in NEAR + FAR[:3]:
+    def y_part(layer, q, up, half):
+        return wts.at[layer, pl.ds(11 * q + (0 if up else 6), 6 if up else 5), pl.ds(4 * half, 4)]
+
+    def along_y(layer, turn):
+        for e, d in NEAR if turn == 0 else FAR[:3]:
             m = peer(e, d)
             arrived(slice_of(layer, m), g_recv.at[layer, m])
-        part = wts.at[layer, half]
+        half = (zh + turn) % 2
+        for up, y in ((1, y_up), (0, y_down)):
+            part = y_part(layer, quarter, up, half)
+            send(part, part, y_send.at[layer, turn, up], y_recv.at[layer, turn, up], (y, n))
+
+    def to_sibling(layer):
+        for turn in range(2):
+            for up in (1, 0):
+                part = y_part(layer, quarter + 1 - 2 * (yy % 2), up, (zh + turn) % 2)
+                arrived(part, y_recv.at[layer, turn, up])
+        part = wts.at[layer, pl.ds(22 * core, 22)]
         send(part, part, c_send.at[layer], c_recv.at[layer], (sibling, n))
 
     to_peers(0)
 
     w1k[...] = jnp.zeros_like(w1k)
 
-    @pl.loop(0, 5)
-    def _(a):
+    def fill(a, odd):
         for b in range(5):
             step, rp = b // 2, b % 2
             at = a * 3 + step
             v = w1_ref[a * 5 + b].astype(F32)
             last = jnp.concatenate([v[96:120], jnp.zeros((8, 192), F32)], axis=0)
-            w1k[at, 48 * rp : 48 * rp + 48, 0:192] = v[0:48].astype(BF16)
-            w1k[at, 128 + 48 * rp : 176 + 48 * rp, 0:192] = v[48:96].astype(BF16)
-            w1k[at, 96 + 128 * rp : 128 + 128 * rp, 0:192] = last.astype(BF16)
+            for base, rows in ((0, v[0:48]), (128, v[48:96])):
+                rows = rows.astype(BF16)
+                if not odd:
+                    w1k[at, base + 48 * rp : base + 48 * rp + 48, 0:192] = rows
+                elif rp == 0:
+                    w1k[at, base + 96 : base + 128, 0:192] = rows[0:32]
+                    w1k[at, base : base + 16, 0:192] = rows[32:48]
+                else:
+                    w1k[at, base + 16 : base + 64, 0:192] = rows
+            gap = 128 * rp + (64 if odd else 96)
+            w1k[at, gap : gap + 32, 0:192] = last.astype(BF16)
+
+    @pl.loop(0, 3)
+    def _(t):
+        fill(2 * t, False)
+
+    @pl.loop(0, 2)
+    def _(t):
+        fill(2 * t + 1, True)
 
     planes[:, 0:16, :] = jnp.zeros((5, 16, 256), BF16)
     planes[:, 528:544, :] = jnp.zeros((5, 16, 256), BF16)
@@ -191,7 +225,7 @@
         four = pl.ds(4 * g, 4)
         send(recv1.at[four], from_lo.at[four], f_send.at[0, turn], f_recv.at[0, g], (hi, n), has_hi)
         send(
-            recv1.at[four, 0], from_hi.at[four], f_send.at[1, turn], f_recv.at[1, g], (lo, n), has_lo
+            recv1.at[four, 0:64], from_hi.at[four], f_send.at[1, turn], f_recv.at[1, g], (lo, n), has_lo
         )
         if turn == 0:
             to_peers(1)
@@ -201,10 +235,15 @@
         def _(step):
             blk = begin + step
             x = read(blk).astype(F32)
-            ln = iota(x.shape, 1)
+            ln = iota((64, 128), 1)
+            kept = ln < 96
+            if a % 2:
+                rest = jnp.concatenate([x[64:], pltpu.roll(x[64:], 64, 1)], axis=0)
+                x = jnp.where(kept, rest, x[:64])
+                kept = (ln < 64) | (ln >= 96)
             after = rows_shifted(x, 1)
-            before = jnp.where(ln < 96, rows_shifted(x, -1), pltpu.roll(after, 96, 1))
-            same = jnp.where(ln < 96, x, pltpu.roll(after, 48, 1))
+            before = jnp.where(kept, rows_shifted(x, -1), pltpu.roll(after, 96, 1))
+            same = jnp.where(kept, x, pltpu.roll(after, 48, 1))
             at = pl.ds(pl.multiple_of(16 + 64 * blk, 16), 64)
             planes[a, at, 0:128] = before.astype(BF16)
             planes[a, at, 128:256] = same.astype(BF16)
@@ -217,8 +256,9 @@
             rows, w1k[3 * a : 3 * a + 3].reshape(768, 256), preferred_element_type=F32
         )
 
-    build(2, lambda blk: recv1[blk, 0])
-    build(3, lambda blk: recv1[blk, 1])
+    along_y(0, 0)
+    build(2, lambda blk: recv1[blk, 0:64])
+    build(3, lambda blk: recv1[blk])
     acc[32:544, :] = product(2) + product(3)
 
     @pl.when(jnp.logical_not(has_lo))
@@ -234,10 +274,13 @@
         four = pl.ds(4 * g, 4)
         arrived(from_lo.at[four], f_recv.at[0, g], has_lo)
         arrived(from_hi.at[four], f_recv.at[1, g], has_hi)
-        if turn == 1:
+        if turn == 0:
             forward(0)
-        build(0, lambda blk: from_lo[blk, 0], 4 * g, 4)
-        build(1, lambda blk: from_lo[blk, 1], 4 * g, 4)
+        else:
+            forward(1)
+            along_y(1, 0)
+        build(0, lambda blk: from_lo[blk, 0:64], 4 * g, 4)
+        build(1, lambda blk: from_lo[blk], 4 * g, 4)
         build(4, lambda blk: from_hi[blk], 4 * g, 4)
         size = (240, 272)[turn]
         first = pl.multiple_of(zh * 272 if turn == 0 else (1 - zh) * 240, 16)
@@ -258,7 +301,8 @@
     for e, d in FAR + NEAR:
         m = peer(e, d)
         send(send2.at[m], recv2.at[n], s2_send.at[m], s2_recv.at[n], (w, m))
-    forward(1)
+    along_y(0, 1)
+    along_y(1, 1)
     to_sibling(0)
 
     total = packed(pl.ds(pl.multiple_of(64 * n, 64), 128))
@@ -328,7 +372,7 @@
 
     lat_p[1] = inside(jnp.abs(latent.astype(F32)), 4 * n - 2)
     exchange(lat_p, l_send, l_recv)
-    other = pl.ds(21 * (1 - core), 21)
+    other = pl.ds(22 * (1 - core), 22)
     arrived(wts.at[0, other], c_recv.at[0])
     to_sibling(1)
     hidden = jnp.maximum(layer_of(0, lat_p, lat_q, l_recv, 96) + b2_ref[...], 0.0)
@@ -367,16 +411,16 @@
             pltpu.VMEM((27, 24, 192), BF16),
             pltpu.VMEM((1, 192), F32),
             dma((9,)),
-            pltpu.VMEM((8, 2, 64, 128), BF16),
-            pltpu.VMEM((8, 2, 64, 128), BF16),
-            pltpu.VMEM((8, 2, 64, 128), BF16),
+            pltpu.VMEM((8, 96, 128), BF16),
+            pltpu.VMEM((8, 96, 128), BF16),
+            pltpu.VMEM((8, 96, 128), BF16),
             pltpu.VMEM((8, 64, 128), BF16),
             pltpu.VMEM((5, 544, 256), BF16),
             pltpu.VMEM((15, 256, 256), BF16),
             pltpu.VMEM((576, 256), F32),
             pltpu.VMEM((8, 192, 128), BF16),
             pltpu.VMEM((8, 192, 128), BF16),
-            pltpu.VMEM((2, 42, 8, 24, 128), BF16),
+            pltpu.VMEM((2, 44, 8, 24, 128), BF16),
             pltpu.VMEM((3, 128, 192), BF16),
             pltpu.VMEM((3, 2, 128, 192), BF16),
             pltpu.VMEM((3, 96, 192), BF16),
@@ -385,6 +429,7 @@
             dma((2, 2)), dma((2, 2)),
             dma((8,)), dma((8,)),
             dma((2, 7)), dma((2, 8)),
+            dma((2, 2, 2)), dma((2, 2, 2)),
             dma((2,)), dma((2,)),
             dma((2,)), dma((2,)),
             dma((2,)), dma((2,)),

time: 56.8 us -> 54.5 us (0.960)
  the two profiles are of different devices: /device:TPU:121 before, /device:TPU:1 now
where the time goes in v3:
time: 54.5 us; the launch traced here: 54.3 us
  Pallas kernels  50.8 us (93%)
  local copies, waits for them, and re-layouts  2.85 us (5%)
  between operations  0.64 us (1%)
    pallas_call x1, Pallas kernels, on_device(): pl.pallas_call(kernel, out_shape=(jax.ShapeDtypeStruct((64, 192), BF16),...  50.8 us
    unnamed x2, local copies, waits for them, and re-layouts  2.85 us

profile of v3, /device:TPU:1, one launch (start us, length us, event | category | flops | bytes accessed | tf_op | source)
XLA Modules:
  0.0 54.3 jit_solution(3301893047808573553)
XLA Ops:
  0.6 50.8 %shard_map.104 = (bf16[64,192]{1,0:T(8,128)(2,1)}, f32[64,192]{1,0:T(8,128)}) custom-call(bf16[512,192]{1,0:T(8,128)(2,1)} %bitcast.13, bf16[25,120,192]{2,1,0:T(8,128)(2,1)} %bitcast.10, f32[1,192]{1,0:T(1,128)} %bitcast.16, f32[1,192]{1,0:T(1,128)} %bitcast.17, f32[192,192]{1,0:T(8,128)} %gamma_in.1, bf16[27,24,192]{2,1,0:T(8,128)(2,1)} %bitcast.11, ...), custom_call_target="tpu_custom_call" | custom-call | tf_op jit(solution)/shard_map/pallas_call | solution.py:395
  51.4 1.4 %copy.13 = bf16[1,4,16,192]{3,2,1,0:T(8,128)(2,1)} copy(bf16[1,4,16,192]{3,2,1,0:T(8,128)(2,1)} %bitcast.15) | data formatting | bytes 49152
  52.8 1.5 %copy.14 = f32[1,4,16,192]{3,2,1,0:T(8,128)} copy(f32[1,4,16,192]{3,2,1,0:T(8,128)} %bitcast.14) | data formatting | bytes 98304

commit v4 on v3

--- a/solution.py
+++ b/solution.py
@@ -11,7 +11,6 @@
 
 FAR = ((1, 2), (1, 1), (1, 3), (1, 0))
 NEAR = ((0, 2), (0, 1), (0, 3))
-TAPS = tuple((a, b, c) for a in range(3) for b in range(3) for c in range(3))
 
 
 def iota(shape, dim):
@@ -95,33 +94,33 @@
     def _():
         pl.semaphore_signal(barrier, inc=1, device_id=(hi, n), device_id_type=MESH)
 
-    loads[0].wait()
     i, j = iota((256, 256), 0), iota((256, 256), 1)
     source = ((i >> 4) & 3) * 64 + (i >> 7) * 32 + (i & 15) * 2 + ((i >> 6) & 1)
     perm = jnp.where(j == source, 1.0, 0.0).astype(BF16)
+    loads[0].wait()
     cut = [
-        jnp.dot(perm, x_ref[256 * z : 256 * z + 256, :], preferred_element_type=F32).astype(BF16)
+        jnp.dot(perm, x_ref[256 * z : 256 * z + 256, :], preferred_element_type=F32)
         for z in range(2)
     ]
     parts = [
         jnp.concatenate([cut[z][64 * t : 64 * t + 64] for z in range(2)], axis=0) for t in range(4)
     ]
-    k, l = iota((192, 256), 0), iota((192, 256), 1)
-    lane, which = l & 127, l >> 7
-    for pair in range(4):
-        total = jnp.zeros((128, 256), F32)
-        for t in range(4):
-            inside = (lane >= 24 * t) & (lane < 24 * t + 24)
-            pick = inside & (k == 24 * (2 * pair + which) + lane - 24 * t)
-            pick = jnp.where(pick, 1.0, 0.0).astype(BF16)
-            total = total + jnp.dot(parts[t], pick, preferred_element_type=F32)
-        for side in range(2):
-            first = total[:64, 128 * side : 128 * side + 128]
-            second = pltpu.roll(total[64:, 128 * side : 128 * side + 128], 96, 1)
-            ln = iota((64, 128), 1)
-            rest = jnp.where(ln[:32] < 64, second[:32], pltpu.roll(second[32:], 64, 1))
-            block = jnp.concatenate([jnp.where(ln < 96, first, second), rest], axis=0)
-            send1[2 * pair + side] = block.astype(BF16)
+    blank = jnp.zeros((128, 64), F32)
+    turned = [
+        pltpu.roll(jnp.concatenate([parts[t], blank], axis=1), 24 * t, 1) if t else
+        jnp.concatenate([parts[t], blank], axis=1)
+        for t in range(4)
+    ]
+    lane = iota((128, 256), 1)
+    for m in range(8):
+        at = (lane - 24 * m) & 255
+        block = jnp.where(at < 24, turned[0], jnp.where(at < 48, turned[1], jnp.where(at < 72, turned[2], turned[3])))
+        block = pltpu.roll(block, (256 - 24 * m) % 256, 1)[:, :128] if m else block[:, :128]
+        block = jnp.where(lane[:, :128] < 96, block, 0.0)
+        first, second = block[:64], pltpu.roll(block[64:], 96, 1)
+        ln = iota((64, 128), 1)
+        rest = jnp.where(ln[:32] < 64, second[:32], pltpu.roll(second[32:], 64, 1))
+        send1[m] = jnp.concatenate([jnp.where(ln < 96, first, second), rest], axis=0).astype(BF16)
 
     pl.semaphore_wait(barrier, 9 + has_lo.astype(jnp.int32) + has_hi.astype(jnp.int32))
 
@@ -183,6 +182,7 @@
         send(part, part, c_send.at[layer], c_recv.at[layer], (sibling, n))
 
     to_peers(0)
+    to_peers(1)
 
     w1k[...] = jnp.zeros_like(w1k)
 
@@ -227,11 +227,9 @@
         send(
             recv1.at[four, 0:64], from_hi.at[four], f_send.at[1, turn], f_recv.at[1, g], (lo, n), has_lo
         )
-        if turn == 0:
-            to_peers(1)
 
     def build(a, read, begin=0, count=8):
-        @pl.loop(0, count)
+        @pl.loop(0, count, unroll=count // 2)
         def _(step):
             blk = begin + step
             x = read(blk).astype(F32)
@@ -338,34 +336,37 @@
 
         sums = [jnp.zeros((rows, 256), F32)] * 2
 
-        def taps(z):
-            for tap in range(9 * z, 9 * z + 9):
-                _, b, c = TAPS[tap]
+        def taps(z, first):
+            for j in range(9):
+                b, c = j // 3, j % 3
                 at = pl.ds(16 * b, rows)
                 left = buf[z, at, :] if c == 1 else buf_q[z, c // 2, at, :]
+                if z is one:
+                    pair, odd = (9 + j) // 2, (9 + j) % 2
+                else:
+                    pair, odd = first + j // 2, j % 2
                 kern = jnp.concatenate(
-                    [kernel_of(layer, 3 * (tap // 2) + tap % 2), kernel_of(layer, 3 * (tap // 2) + 2)],
-                    axis=1,
+                    [kernel_of(layer, 3 * pair + odd), kernel_of(layer, 3 * pair + 2)], axis=1
                 )
-                sums[tap % 2] += jnp.dot(left, kern, preferred_element_type=F32)
-
-        shifts(1)
-        taps(1)
-
-        @pl.when(jnp.logical_not(has_lo))
+                sums[odd] += jnp.dot(left, kern, preferred_element_type=F32)
+
+        one = 1
+        shifts(one)
+        taps(one, None)
+        near = 2 * (1 - core)
+        far = 2 - near
+        has_far = jnp.where(core == 0, has_lo.astype(jnp.int32), has_hi.astype(jnp.int32)) == 1
+
+        @pl.when(jnp.logical_not(has_far))
         def _():
-            buf[0] = jnp.zeros_like(buf[0])
-
-        @pl.when(jnp.logical_not(has_hi))
-        def _():
-            buf[2] = jnp.zeros_like(buf[2])
-
-        arrived(buf.at[0], rsem.at[0], has_lo)
-        shifts(0)
-        taps(0)
-        arrived(buf.at[2], rsem.at[1], has_hi)
-        shifts(2)
-        taps(2)
+            buf[far] = jnp.zeros((buf.shape[1], 192), BF16)
+
+        arrived(buf.at[near], rsem.at[1 - core])
+        shifts(near)
+        taps(near, 9 * (1 - core))
+        arrived(buf.at[far], rsem.at[core], has_far)
+        shifts(far)
+        taps(far, 9 * core)
         even, odd = sums
         side = even[:, 128:] + pltpu.roll(odd[:, 128:], 64, 1)
         return jnp.concatenate([even[:, :128] + odd[:, :128], side[:, :64]], axis=1)

time: 54.5 us -> 52.5 us (0.963)
  the two profiles are of different devices: /device:TPU:1 before, /device:TPU:121 now
where the time goes in v4:
time: 52.5 us; the launch traced here: 52.3 us
  Pallas kernels  48.8 us (93%)
  local copies, waits for them, and re-layouts  2.85 us (5%)
  between operations  0.64 us (1%)
    pallas_call x1, Pallas kernels, on_device(): pl.pallas_call(kernel, out_shape=(jax.ShapeDtypeStruct((64, 192), BF16),...  48.8 us
    unnamed x2, local copies, waits for them, and re-layouts  2.85 us

profile of v4, /device:TPU:121, one launch (start us, length us, event | category | flops | bytes accessed | tf_op | source)
XLA Modules:
  0.0 52.3 jit_solution(4456457830463223538)
XLA Ops:
  0.6 48.8 %shard_map.104 = (bf16[64,192]{1,0:T(8,128)(2,1)}, f32[64,192]{1,0:T(8,128)}) custom-call(bf16[512,192]{1,0:T(8,128)(2,1)} %bitcast.13, bf16[25,120,192]{2,1,0:T(8,128)(2,1)} %bitcast.10, f32[1,192]{1,0:T(1,128)} %bitcast.16, f32[1,192]{1,0:T(1,128)} %bitcast.17, f32[192,192]{1,0:T(8,128)} %gamma_in.1, bf16[27,24,192]{2,1,0:T(8,128)(2,1)} %bitcast.11, ...), custom_call_target="tpu_custom_call" | custom-call | tf_op jit(solution)/shard_map/pallas_call | solution.py:396
  49.4 1.4 %copy.13 = bf16[1,4,16,192]{3,2,1,0:T(8,128)(2,1)} copy(bf16[1,4,16,192]{3,2,1,0:T(8,128)(2,1)} %bitcast.15) | data formatting | bytes 49152
  50.8 1.5 %copy.14 = f32[1,4,16,192]{3,2,1,0:T(8,128)} copy(f32[1,4,16,192]{3,2,1,0:T(8,128)} %bitcast.14) | data formatting | bytes 98304

commit v5 on v4

--- a/solution.py
+++ b/solution.py
@@ -41,8 +41,7 @@
             (b1_in, b1_ref), (beta_in, beta_ref), (b2_in, b2_ref), (b3_in, b3_ref),
         ))
     ]
-    for load in loads:
-        load.start()
+    loads[0].start()
     w, n = lax.axis_index("wide"), lax.axis_index("narrow")
     wide = lax.axis_size("wide")
     zh, xx, core = n // 4, n % 4, w % 2
@@ -98,6 +97,8 @@
     source = ((i >> 4) & 3) * 64 + (i >> 7) * 32 + (i & 15) * 2 + ((i >> 6) & 1)
     perm = jnp.where(j == source, 1.0, 0.0).astype(BF16)
     loads[0].wait()
+    for load in loads[1:]:
+        load.start()
     cut = [
         jnp.dot(perm, x_ref[256 * z : 256 * z + 256, :], preferred_element_type=F32)
         for z in range(2)
@@ -274,9 +275,6 @@
         arrived(from_hi.at[four], f_recv.at[1, g], has_hi)
         if turn == 0:
             forward(0)
-        else:
-            forward(1)
-            along_y(1, 0)
         build(0, lambda blk: from_lo[blk, 0:64], 4 * g, 4)
         build(1, lambda blk: from_lo[blk], 4 * g, 4)
         build(4, lambda blk: from_hi[blk], 4 * g, 4)
@@ -292,13 +290,12 @@
         side = jnp.where(ln < 64, right[:64], pltpu.roll(right[64:], 64, 1))
         return jnp.concatenate([left, side], axis=0)
 
-    @pl.loop(0, 8)
-    def _(m):
-        send2[m] = packed(pl.ds(pl.multiple_of(64 * m, 64), 128)).astype(BF16)
-
     for e, d in FAR + NEAR:
         m = peer(e, d)
+        send2[m] = packed(pl.ds(pl.multiple_of(64 * m, 64), 128)).astype(BF16)
         send(send2.at[m], recv2.at[n], s2_send.at[m], s2_recv.at[n], (w, m))
+    forward(1)
+    along_y(1, 0)
     along_y(0, 1)
     along_y(1, 1)
     to_sibling(0)
@@ -315,7 +312,6 @@
         conv * conv, gamma_ref[...], precision=lax.Precision.HIGHEST, preferred_element_type=F32
     )
     latent = (conv * lax.rsqrt(denom)).astype(BF16)
-    lat_ref[...] = latent[32:96]
 
     def inside(values, first):
         row = first + (iota(values.shape, 0) >> 4)
@@ -364,6 +360,8 @@
         arrived(buf.at[near], rsem.at[1 - core])
         shifts(near)
         taps(near, 9 * (1 - core))
+        if layer == 0:
+            to_sibling(1)
         arrived(buf.at[far], rsem.at[core], has_far)
         shifts(far)
         taps(far, 9 * core)
@@ -373,21 +371,27 @@
 
     lat_p[1] = inside(jnp.abs(latent.astype(F32)), 4 * n - 2)
     exchange(lat_p, l_send, l_recv)
+    lat_ref[...] = latent[32:96]
     other = pl.ds(22 * (1 - core), 22)
     arrived(wts.at[0, other], c_recv.at[0])
-    to_sibling(1)
     hidden = jnp.maximum(layer_of(0, lat_p, lat_q, l_recv, 96) + b2_ref[...], 0.0)
     hid_p[1] = inside(hidden, 4 * n - 1)
     exchange(hid_p, h_send, h_recv)
     arrived(wts.at[1, other], c_recv.at[1])
     s = layer_of(1, hid_p, hid_q, h_recv, 64) + b3_ref[...]
-    sc_ref[...] = 0.11 + (jnp.maximum(s, 0.0) + jnp.log1p(jnp.exp(-jnp.abs(s))))
+    sc_ref[...] = s
 
     for copy, when in sent:
         if when is None:
             copy.wait_send()
         else:
             pl.when(when)(copy.wait_send)
+
+
+def finish(lat_in, s_in, lat_ref, sc_ref):
+    lat_ref[...] = lat_in[...]
+    s = s_in[...]
+    sc_ref[...] = 0.11 + (jnp.maximum(s, 0.0) + jnp.log1p(jnp.exp(-jnp.abs(s))))
 
 
 def on_device(density, w1, b1, beta, gamma, w2, b2, w3, b3):
@@ -449,6 +453,15 @@
         w3.reshape(27, 24, 192),
         b3.reshape(1, 192),
     )
+    latent, scales = pl.pallas_call(
+        finish,
+        out_shape=(
+            jax.ShapeDtypeStruct((64, 192), BF16),
+            jax.ShapeDtypeStruct((64, 192), F32),
+        ),
+        in_specs=[vmem] * 2,
+        out_specs=(vmem, vmem),
+    )(latent, scales)
     return latent.reshape(1, 4, 16, 192), scales.reshape(1, 4, 16, 192)
 
 

time: 52.5 us -> 50.8 us (0.968)
  the two profiles are of different devices: /device:TPU:121 before, /device:TPU:1 now
where the time goes in v5:
time: 50.8 us; the launch traced here: 50.6 us
  Pallas kernels  49.9 us (98%)
  between operations  0.64 us (1%)
    pallas_call x1, Pallas kernels, on_device(): pl.pallas_call(kernel, out_shape=(jax.ShapeDtypeStruct((64, 192), BF16),...  48.4 us
    pallas_call x1, Pallas kernels, on_device(): pl.pallas_call(finish, out_shape=(jax.ShapeDtypeStruct((64, 192), BF16),...  1.54 us

profile of v5, /device:TPU:1, one launch (start us, length us, event | category | flops | bytes accessed | tf_op | source)
XLA Modules:
  0.0 50.6 jit_solution(2473478573240032316)
XLA Ops:
  0.6 48.4 %shard_map.104 = (bf16[64,192]{1,0:T(8,128)(2,1)}, f32[64,192]{1,0:T(8,128)}) custom-call(bf16[512,192]{1,0:T(8,128)(2,1)} %bitcast.13, bf16[25,120,192]{2,1,0:T(8,128)(2,1)} %bitcast.10, f32[1,192]{1,0:T(1,128)} %bitcast.14, f32[1,192]{1,0:T(1,128)} %bitcast.15, f32[192,192]{1,0:T(8,128)} %gamma_in.1, bf16[27,24,192]{2,1,0:T(8,128)(2,1)} %bitcast.11, ...), custom_call_target="tpu_custom_call" | custom-call | tf_op jit(solution)/shard_map/pallas_call | solution.py:400
  49.0 1.5 %shard_map.105 = (bf16[64,192]{1,0:T(8,128)(2,1)}, f32[64,192]{1,0:T(8,128)}) custom-call(bf16[64,192]{1,0:T(8,128)(2,1)} %get-tuple-element.6.lat_in, f32[64,192]{1,0:T(8,128)} %get-tuple-element.7.s_in), custom_call_target="tpu_custom_call" | custom-call | tf_op jit(solution)/shard_map/pallas_call | solution.py:456

commit v6 on v5

--- a/solution.py
+++ b/solution.py
@@ -133,10 +133,10 @@
     for load in loads[1:]:
         load.wait()
 
-    for layer, ref in ((0, w2_ref), (1, w3_ref)):
+    def stage(layer, ref):
 
         @pl.loop(0, 11)
-        def _(t, layer=layer, ref=ref):
+        def _(t):
             at = 11 * quarter + t
             tap, kind = 2 * (at // 3), at % 3
             even = ref[jnp.minimum(tap, 26)].astype(F32)
@@ -182,8 +182,9 @@
         part = wts.at[layer, pl.ds(22 * core, 22)]
         send(part, part, c_send.at[layer], c_recv.at[layer], (sibling, n))
 
-    to_peers(0)
-    to_peers(1)
+    for layer, ref in ((0, w2_ref), (1, w3_ref)):
+        stage(layer, ref)
+        to_peers(layer)
 
     w1k[...] = jnp.zeros_like(w1k)
 
@@ -271,17 +272,32 @@
     for turn in range(2):
         g = (zh + turn) % 2
         four = pl.ds(4 * g, 4)
-        arrived(from_lo.at[four], f_recv.at[0, g], has_lo)
-        arrived(from_hi.at[four], f_recv.at[1, g], has_hi)
         if turn == 0:
             forward(0)
-        build(0, lambda blk: from_lo[blk, 0:64], 4 * g, 4)
-        build(1, lambda blk: from_lo[blk], 4 * g, 4)
-        build(4, lambda blk: from_hi[blk], 4 * g, 4)
         size = (240, 272)[turn]
         first = pl.multiple_of(zh * 272 if turn == 0 else (1 - zh) * 240, 16)
-        add = product(0, first, size) + product(1, first, size) + product(4, first, size)
-        acc[pl.ds(pl.multiple_of(32 + first, 16), size), :] += add
+        target = pl.ds(pl.multiple_of(32 + first, 16), size)
+
+        def use_lo(g=g, four=four, first=first, size=size, target=target):
+            arrived(from_lo.at[four], f_recv.at[0, g], has_lo)
+            build(0, lambda blk: from_lo[blk, 0:64], 4 * g, 4)
+            build(1, lambda blk: from_lo[blk], 4 * g, 4)
+            acc[target, :] += product(0, first, size) + product(1, first, size)
+
+        def use_hi(g=g, four=four, first=first, size=size, target=target):
+            arrived(from_hi.at[four], f_recv.at[1, g], has_hi)
+            build(4, lambda blk: from_hi[blk], 4 * g, 4)
+            acc[target, :] += product(4, first, size)
+
+        @pl.when(core == 0)
+        def _():
+            use_hi()
+            use_lo()
+
+        @pl.when(core == 1)
+        def _():
+            use_lo()
+            use_hi()
 
     def packed(at):
         rows = acc[at, :]

time: 50.8 us -> 50.5 us (level); the launches traced: 50.6 us -> 49.6 us
  Pallas kernels: 49.9 us -> 49 us
    pallas_call x1, Pallas kernels: 48.4 us -> 47.5 us  [on_device(): pl.pallas_call(kernel, out_shape=(jax.ShapeDtypeStruct((64, 192), BF16),...]
where the time goes in v6:
time: 50.5 us; the launch traced here: 49.6 us
  Pallas kernels  49 us (97%)
  between operations  0.64 us (1%)
    pallas_call x1, Pallas kernels, on_device(): pl.pallas_call(kernel, out_shape=(jax.ShapeDtypeStruct((64, 192), BF16),...  47.5 us
    pallas_call x1, Pallas kernels, on_device(): pl.pallas_call(finish, out_shape=(jax.ShapeDtypeStruct((64, 192), BF16),...  1.54 us

profile of v6, /device:TPU:1, one launch (start us, length us, event | category | flops | bytes accessed | tf_op | source)
XLA Modules:
  0.0 49.6 jit_solution(8156468857167152518)
XLA Ops:
  0.6 47.5 %shard_map.104 = (bf16[64,192]{1,0:T(8,128)(2,1)}, f32[64,192]{1,0:T(8,128)}) custom-call(bf16[512,192]{1,0:T(8,128)(2,1)} %bitcast.13, bf16[25,120,192]{2,1,0:T(8,128)(2,1)} %bitcast.10, f32[1,192]{1,0:T(1,128)} %bitcast.14, f32[1,192]{1,0:T(1,128)} %bitcast.15, f32[192,192]{1,0:T(8,128)} %gamma_in.1, bf16[27,24,192]{2,1,0:T(8,128)(2,1)} %bitcast.11, ...), custom_call_target="tpu_custom_call" | custom-call | tf_op jit(solution)/shard_map/pallas_call | solution.py:416
  48.1 1.5 %shard_map.105 = (bf16[64,192]{1,0:T(8,128)(2,1)}, f32[64,192]{1,0:T(8,128)}) custom-call(bf16[64,192]{1,0:T(8,128)(2,1)} %get-tuple-element.6.lat_in, f32[64,192]{1,0:T(8,128)} %get-tuple-element.7.s_in), custom_call_target="tpu_custom_call" | custom-call | tf_op jit(solution)/shard_map/pallas_call | solution.py:472

commit v7 on v5

--- a/solution.py
+++ b/solution.py
@@ -133,10 +133,10 @@
     for load in loads[1:]:
         load.wait()
 
-    for layer, ref in ((0, w2_ref), (1, w3_ref)):
+    def stage(layer, ref):
 
         @pl.loop(0, 11)
-        def _(t, layer=layer, ref=ref):
+        def _(t):
             at = 11 * quarter + t
             tap, kind = 2 * (at // 3), at % 3
             even = ref[jnp.minimum(tap, 26)].astype(F32)
@@ -182,8 +182,9 @@
         part = wts.at[layer, pl.ds(22 * core, 22)]
         send(part, part, c_send.at[layer], c_recv.at[layer], (sibling, n))
 
-    to_peers(0)
-    to_peers(1)
+    for layer, ref in ((0, w2_ref), (1, w3_ref)):
+        stage(layer, ref)
+        to_peers(layer)
 
     w1k[...] = jnp.zeros_like(w1k)
 

time: 50.8 us -> 51.1 us (level)
  no operation moved by 1% of the time
where the time goes in v7:
time: 51.1 us; the launch traced here: 50.4 us
  Pallas kernels  49.8 us (97%)
  between operations  0.64 us (1%)
    pallas_call x1, Pallas kernels, on_device(): pl.pallas_call(kernel, out_shape=(jax.ShapeDtypeStruct((64, 192), BF16),...  48.2 us
    pallas_call x1, Pallas kernels, on_device(): pl.pallas_call(finish, out_shape=(jax.ShapeDtypeStruct((64, 192), BF16),...  1.54 us

profile of v7, /device:TPU:1, one launch (start us, length us, event | category | flops | bytes accessed | tf_op | source)
XLA Modules:
  0.0 50.4 jit_solution(9627647310832205505)
XLA Ops:
  0.6 48.2 %shard_map.104 = (bf16[64,192]{1,0:T(8,128)(2,1)}, f32[64,192]{1,0:T(8,128)}) custom-call(bf16[512,192]{1,0:T(8,128)(2,1)} %bitcast.13, bf16[25,120,192]{2,1,0:T(8,128)(2,1)} %bitcast.10, f32[1,192]{1,0:T(1,128)} %bitcast.14, f32[1,192]{1,0:T(1,128)} %bitcast.15, f32[192,192]{1,0:T(8,128)} %gamma_in.1, bf16[27,24,192]{2,1,0:T(8,128)(2,1)} %bitcast.11, ...), custom_call_target="tpu_custom_call" | custom-call | tf_op jit(solution)/shard_map/pallas_call | solution.py:401
  48.9 1.5 %shard_map.105 = (bf16[64,192]{1,0:T(8,128)(2,1)}, f32[64,192]{1,0:T(8,128)}) custom-call(bf16[64,192]{1,0:T(8,128)(2,1)} %get-tuple-element.6.lat_in, f32[64,192]{1,0:T(8,128)} %get-tuple-element.7.s_in), custom_call_target="tpu_custom_call" | custom-call | tf_op jit(solution)/shard_map/pallas_call | solution.py:457
